TPU v7x, 32 devices: a whole 2x2x4 slice. The times are simulated.
32 devices in a mesh: dp: 4 (over y, core), fsdp: 8 (over z, x).
Axes of the slice: x: 2, y: 2, z: 4, core: 2. Of those that a mesh axis runs over, the one named last changes fastest.
Arguments:
- tokens: bfloat16 [32, 1024, 768], P(('dp', 'fsdp')), may hold values from -36 to 36
- cotangent: bfloat16 [32, 1024, 768], P(('dp', 'fsdp')), may hold values from -6 to 6
- document_ids: int32 [32, 1024], P(('dp', 'fsdp')), may hold values from 0 to 3, never falling along the last dimension, each value on 1 to 512 neighbouring positions
- source_layer: int32 [], replicated, may hold values from 0 to 11
- attngain: bfloat16 [12, 768], P(None, ('dp', 'fsdp')), may hold values from 0.5 to 1.5
- attnshift: bfloat16 [12, 768], P(None, ('dp', 'fsdp')), may hold values from -3 to 3
- qkvmatrix: bfloat16 [12, 768, 2304], P(None, ('dp', 'fsdp')), may hold values from -0.21875 to 0.21875
- qvoffset: bfloat16 [12, 1536], P(None, ('dp', 'fsdp')), may hold values from -3 to 3
- outmatrix: bfloat16 [12, 768, 768], P(None, ('dp', 'fsdp')), may hold values from -0.875 to 0.875
- outoffset: bfloat16 [12, 768], P(None, ('dp', 'fsdp')), may hold values from -3 to 3
- mlpgain: bfloat16 [12, 768], P(None, ('dp', 'fsdp')), may hold values from 0.5 to 1.5
- mlpshift: bfloat16 [12, 768], P(None, ('dp', 'fsdp')), may hold values from -3 to 3
- upmatrix: bfloat16 [12, 768, 3072], P(None, ('dp', 'fsdp')), may hold values from -0.21875 to 0.21875
- upoffset: bfloat16 [12, 3072], P(None, ('dp', 'fsdp')), may hold values from -3 to 3
- downmatrix: bfloat16 [12, 3072, 768], P(None, ('dp', 'fsdp')), may hold values from -0.109375 to 0.109375
- downoffset: bfloat16 [12, 768], P(None, ('dp', 'fsdp')), may hold values from -3 to 3
Outputs:
- layer_output: float32 [32, 1024, 768], P(('dp', 'fsdp'))
- input_grad: float32 [32, 1024, 768], P(('dp', 'fsdp'))
- attngain_grad: float32 [768], P(('dp', 'fsdp'))
- attnshift_grad: float32 [768], P(('dp', 'fsdp'))
- qkvmatrix_grad: float32 [768, 2304], P(('dp', 'fsdp'))
- qvoffset_grad: float32 [1536], P(('dp', 'fsdp'))
- outmatrix_grad: float32 [768, 768], P(('dp', 'fsdp'))
- outoffset_grad: float32 [768], P(('dp', 'fsdp'))
- mlpgain_grad: float32 [768], P(('dp', 'fsdp'))
- mlpshift_grad: float32 [768], P(('dp', 'fsdp'))
- upmatrix_grad: float32 [768, 3072], P(('dp', 'fsdp'))
- upoffset_grad: float32 [3072], P(('dp', 'fsdp'))
- downmatrix_grad: float32 [3072, 768], P(('dp', 'fsdp'))
- downoffset_grad: float32 [768], P(('dp', 'fsdp'))
Inputs may be any that keep to these rules, and one draw needn't show every extreme that they name: `document_ids`: in each packed row the document numbers start at 0 and never fall; a document holds at most 512 tokens, and one of each row holds exactly that many.
All inputs are finite; a program needn't handle non-finite values.
Results may differ from a plain program's by a relative error of at most 0.0095.
Values may be sent and summed in bfloat16 or wider, within the bound.
A program may use at most 256 MiB of HBM per device.

v0:
```python
import functools

import jax
import jax.numpy as jnp
from jax import lax
from jax.experimental import pallas as pl
from jax.experimental.pallas import tpu as pltpu
from jax.sharding import PartitionSpec as P

MESH = pl.DeviceIdType.MESH
F32 = jnp.float32
BF = jnp.bfloat16
EPSILON = 1e-05
NEG_LARGE = -1000000000.0
GELU_COEF = 0.7978845608028654
GELU_CUBIC = 0.044715
WIDTH = 768
HALF = 384
HEAD = 64
QB = 256
VEC_ROWS = 8
VMEM_BYTES = 63 * 2**20
VEC_SIZES = (1, 1, 2, 1, 1, 1, 4, 1)
OUT, UNITS = 3, 12


def up(quarter):
    return OUT + 1 + 2 * quarter


def down(quarter):
    return OUT + 2 + 2 * quarter


SCHEDULE = {
    "rows": {
        0: ((0, 0, 2),),
    },
    "att0": {
        0: ((0, 1, 2), (0, 0, 3), (0, 2, 2), (0, 1, 3), (0, 3, 2), (0, 0, 4), (0, 2, 3),),
    },
    "att2": {
        0: ((0, 4, 2),),
        1: ((0, 1, 4), (0, 3, 3), (0, 5, 2),),
        2: ((0, 4, 3),),
        3: ((0, 7, 2),),
        4: ((0, 5, 3), (0, 6, 3), (0, 8, 2),),
        5: ((0, 9, 2),),
    },
    "att1": {
        1: ((0, 2, 4), (0, 6, 2),),
        2: ((0, 3, 4),),
    },
    "attended": {
        0: ((0, 4, 4), (0, 10, 2),),
    },
    "masksT": {
        0: ((0, 7, 3),),
    },
    "ff0": {
        0: ((0, 11, 2), (0, 5, 4),),
        1: ((0, 7, 4), (1, 5, 2), (0, 11, 3), (1, 4, 2),),
    },
    "ff1": {
        1: ((0, 6, 4),),
        3: ((0, 8, 4),),
        4: ((1, 7, 2), (1, 5, 3),),
        5: ((1, 6, 2),),
        6: ((1, 7, 3), (1, 5, 4), (1, 9, 2),),
        7: ((1, 8, 2),),
    },
    "ff3": {
        0: ((0, 8, 3), (0, 9, 3),),
        1: ((0, 9, 4),),
        2: ((0, 11, 4),),
        3: ((1, 4, 4), (1, 6, 3),),
    },
    "ff4": {
        0: ((0, 10, 3),),
        2: ((1, 4, 3),),
        3: ((1, 7, 4), (1, 5, 5),),
    },
    "ff5": {
        1: ((0, 10, 4),),
        3: ((1, 9, 3),),
    },
    "back_two": {
        0: ((1, 11, 2), (1, 8, 3), (1, 10, 2), (1, 4, 5),),
    },
    "back_out": {
        0: ((1, 6, 4), (1, 7, 5),),
    },
    "dWo": {
        0: ((1, 9, 4),),
    },
    "ab0": {
        0: ((1, 11, 3), (1, 3, 2), (1, 8, 4),),
        1: ((1, 10, 3), (1, 6, 5), (1, 9, 5),),
        2: ((1, 3, 3), (1, 0, 2), (1, 8, 5),),
        3: ((1, 10, 4), (1, 11, 5),),
        4: ((1, 0, 3), (1, 1, 2),),
        5: ((1, 10, 5),),
    },
    "ab2": {
        0: ((1, 11, 4),),
        1: ((1, 3, 4),),
        2: ((1, 0, 4), (1, 3, 5),),
    },
    "da1": {
        0: ((1, 1, 3),),
        1: ((1, 2, 2),),
    },
    "back_one": {
        0: ((1, 1, 4), (1, 0, 5),),
    },
    "drain": {
        0: ((1, 2, 3), (1, 1, 5), (1, 2, 4), (1, 2, 5),),
    },
}


def dg(left, right, left_dim, right_dim):
    return lax.dot_general(
        left, right, (((left_dim,), (right_dim,)), ((), ())), preferred_element_type=F32
    )


def mm(left, right):
    return jnp.dot(left, right, preferred_element_type=F32)


def regroup(rows, back):
    to = lax.broadcasted_iota(jnp.int32, (HALF, HALF), 1).astype(F32)
    source = lax.broadcasted_iota(jnp.int32, (HALF, HALF), 0).astype(F32)
    if back:
        to, source = source, to
    high = jnp.floor((to + 0.5) * (1 / (4 * rows)))
    rest = to - 4 * rows * high
    middle = jnp.floor((rest + 0.5) * (1 / rows))
    return source == 4 * rows * middle + rows * high + (rest - rows * middle)


def pack_kernel(layer_ref, *refs):
    vec_in, (qkv, out, up_in, down_in), units, vec_out = refs[:8], refs[8:12], refs[12], refs[13]
    layer = layer_ref[0]
    for t in range(3):
        for part in range(3):
            units[t, :, 256 * part : 256 * part + 256] = qkv[
                0, :, WIDTH * part + 256 * t : WIDTH * part + 256 * t + 256
            ]
    units[OUT] = out[0]
    rows = units.shape[1]
    shards = WIDTH // rows
    wide = up_in[0].astype(F32)
    groups = [wide[:, HALF * g : HALF * g + HALF] for g in range(shards // 4)]
    moved = mm(jnp.concatenate(groups, 0).astype(BF), regroup(rows, False).astype(BF))
    for j in range(4):
        lanes = slice(4 * rows * j, 4 * rows * j + 4 * rows)
        pieces = [moved[rows * g : rows * g + rows, lanes] for g in range(shards // 4)]
        units[up(j)] = jnp.concatenate(pieces, 1).astype(BF)
    wide = down_in[0].astype(F32)
    for j in range(4):
        units[down(j)] = wide[rows * j : rows * j + rows].astype(BF)
    vec_out[...] = jnp.zeros_like(vec_out)
    for r, ref in enumerate(vec_in):
        stack = ref[...].astype(F32)
        index = lax.broadcasted_iota(jnp.int32, stack.shape, 0)
        row = jnp.sum(jnp.where(index == layer, stack, 0.0), axis=0, keepdims=True)
        vec_out[r : r + 1, 0 : stack.shape[1]] = row


def pack_layer(layer, vectors, matrices):
    rows = matrices[0].shape[1]
    whole = [pl.BlockSpec(v.shape, lambda i, s: (0, 0)) for v in vectors]
    picked = [
        pl.BlockSpec((1,) + m.shape[1:], lambda i, s: (s[0], 0, 0)) for m in matrices
    ]
    return pl.pallas_call(
        pack_kernel,
        grid_spec=pltpu.PrefetchScalarGridSpec(
            num_scalar_prefetch=1,
            grid=(1,),
            in_specs=whole + picked,
            out_specs=[
                pl.BlockSpec((UNITS, rows, WIDTH), lambda i, s: (0, 0, 0)),
                pl.BlockSpec((VEC_ROWS, 128), lambda i, s: (0, 0)),
            ],
        ),
        out_shape=[
            jax.ShapeDtypeStruct((UNITS, rows, WIDTH), BF),
            jax.ShapeDtypeStruct((VEC_ROWS, 128), F32),
        ],
        name="pick_layer",
    )(layer.reshape(1), *vectors, *matrices)


def vector_parts(shards):
    base = WIDTH // shards
    parts = {}
    for r, size in enumerate(VEC_SIZES):
        for j in range(4 if size == 4 else 1):
            width = base * (1 if size == 4 else size)
            parts.setdefault(width, []).append((r, base * j, WIDTH * j))
    return parts


def page_maps(shards, width):
    total = shards * width
    col = lax.broadcasted_iota(jnp.int32, (128, total), 1).astype(F32)
    place = lax.broadcasted_iota(jnp.int32, (128, total), 0).astype(F32)
    one_hot = (col - jnp.floor((col + 0.5) * (1 / width)) * width) == place
    col_s = lax.broadcasted_iota(jnp.int32, (shards, total), 1)
    first = lax.broadcasted_iota(jnp.int32, (shards, total), 0) * width
    return one_hot, (col_s >= first) & (col_s < first + width)


def pages_to_rows(pages, fvec, shards):
    for width, parts in vector_parts(shards).items():
        one_hot, mine = page_maps(shards, width)
        one_hot = one_hot.astype(BF)
        for r, lane, start in parts:
            page = pages[:, r, :]
            if lane:
                page = pltpu.roll(page, 128 - lane, 1)
            spread = mm(page.astype(BF), one_hot)
            fvec[r : r + 1, start : start + shards * width] = jnp.sum(
                jnp.where(mine, spread, 0.0), axis=0, keepdims=True
            )


def rows_to_pages(svec, pages, shards):
    for width, parts in vector_parts(shards).items():
        one_hot, mine = page_maps(shards, width)
        one_hot = one_hot.astype(BF)
        for r, lane, start in parts:
            spread = jnp.where(mine, svec[r : r + 1, start : start + shards * width], 0.0)
            high = spread.astype(BF)
            low = (spread - high.astype(F32)).astype(BF)
            page = dg(high, one_hot, 1, 1) + dg(low, one_hot, 1, 1)
            if lane:
                pages[:, r, :] = pages[:, r, :] + pltpu.roll(page, lane, 1)
            else:
                pages[:, r, :] = page


def norm_stats(values):
    mean = jnp.mean(values, axis=-1, keepdims=True)
    centred = values - mean
    spread = jnp.mean(centred * centred, axis=-1, keepdims=True)
    scale = lax.rsqrt(spread + EPSILON)
    return centred * scale, scale


def norm_back(grad, gain, normed, scale):
    scaled = grad * gain
    mean_one = jnp.mean(scaled, axis=-1, keepdims=True)
    mean_two = jnp.mean(scaled * normed, axis=-1, keepdims=True)
    return scale * (scaled - mean_one - normed * mean_two)


def key_ranges(length):
    reach = length // 2
    return [(max(0, i * QB - reach), (i + 1) * QB) for i in range(length // QB)]


def mask_blocks(length):
    blocks = {}
    for i, (lo, hi) in enumerate(key_ranges(length)):
        for key in range(lo, hi, QB):
            blocks[i, key // QB] = len(blocks)
    return blocks


def build_masks(doc_ref, masks, transposed):
    length = doc_ref.shape[1]
    row = doc_ref[...].astype(F32)
    for (i, b), at in mask_blocks(length).items():
        queries = row[:, i * QB : (i + 1) * QB]
        keys = row[:, b * QB : (b + 1) * QB]
        along, down = (queries, keys) if transposed else (keys, queries)
        down = jnp.transpose(jnp.broadcast_to(down, (128, QB)))
        down = jnp.concatenate([down, down], 1)
        q_dim = 1 if transposed else 0
        q_pos = lax.broadcasted_iota(jnp.int32, (QB, QB), q_dim) + i * QB
        k_pos = lax.broadcasted_iota(jnp.int32, (QB, QB), 1 - q_dim) + b * QB
        masks[at] = jnp.where((k_pos <= q_pos) & (down == along), 0.0, NEG_LARGE)


def head_lanes(values, head, other=0.0):
    lane = lax.broadcasted_iota(jnp.int32, values.shape, 1)
    keep = lane >= HEAD if head else lane < HEAD
    return jnp.where(keep, values, jnp.full(values.shape, other, values.dtype))


def pair_lanes(unit, half):
    start = [unit * WIDTH + 256 * part + 128 * half for part in range(3)]
    return [pl.ds(pl.multiple_of(s, 128), 128) for s in start]


def forward_pair(unit, half, qkv, mixed, lse, masks):
    length = qkv.shape[0]
    lanes_q, lanes_k, lanes_v = pair_lanes(unit, half)
    ranges, blocks = key_ranges(length), mask_blocks(length)
    pair = 2 * unit + half
    lanes_o = pl.ds(pl.multiple_of(pair * 128, 128), 128)
    steps = [(i, h) for i in range(len(ranges)) for h in range(2)]

    def scores(step):
        i, h = step
        lo, hi = ranges[i]
        rows = slice(i * QB, (i + 1) * QB)
        raw = dg(head_lanes(qkv[rows, lanes_q], h), qkv[lo:hi, lanes_k], 1, 1)
        mask = [masks[blocks[i, b]] for b in range(lo // QB, hi // QB)]
        return raw + jnp.concatenate(mask, 1)

    def finish(step, score):
        i, h = step
        lo, hi = ranges[i]
        top = jnp.max(score, axis=1, keepdims=True)
        soft = jnp.exp(score - top).astype(BF)
        return mm(soft, head_lanes(qkv[lo:hi, lanes_v], h, 1.0)), top

    current, done = scores(steps[0]), {}
    for n, step in enumerate(steps):
        following = scores(steps[n + 1]) if n + 1 < len(steps) else None
        done[step] = finish(step, current)
        current = following
        i, h = step
        if h == 1:
            (acc0, top0), (acc1, top1) = done.pop((i, 0)), done.pop((i, 1))
            rows = slice(i * QB, (i + 1) * QB)
            first = lax.broadcasted_iota(jnp.int32, acc0.shape, 1) < HEAD
            total = pltpu.roll(jnp.where(first, acc1, acc0), HEAD, 1)
            mixed[rows, lanes_o] = (jnp.where(first, acc0, acc1) / total).astype(BF)
            logs = jnp.transpose(jnp.where(first, top0, top1) + jnp.log(total))
            lse[pair, 0:1, rows] = logs[0:1]
            lse[pair, 1:2, rows] = logs[HEAD : HEAD + 1]


def backward_pair(unit, half, qkv, mixed, mixed_grad, lse, masks, key_acc, value_acc):
    length = qkv.shape[0]
    lanes_q, lanes_k, lanes_v = pair_lanes(unit, half)
    ranges, blocks = key_ranges(length), mask_blocks(length)
    pair = 2 * unit + half
    lanes_o = pl.ds(pl.multiple_of(pair * 128, 128), 128)
    keys_t = jnp.transpose(qkv[:, lanes_k])
    steps = [(i, h) for i in range(len(ranges)) for h in range(2)]
    products = {}

    def start(step):
        i, h = step
        lo, hi = ranges[i]
        rows = slice(i * QB, (i + 1) * QB)
        query = head_lanes(qkv[rows, lanes_q], h)
        grad = head_lanes(mixed_grad[rows, lanes_o], h)
        mask = [masks[blocks[i, b]] for b in range(lo // QB, hi // QB)]
        score = dg(qkv[lo:hi, lanes_k], query, 1, 1) + jnp.concatenate(mask, 0)
        return score, dg(qkv[lo:hi, lanes_v], grad, 1, 1), query, grad

    def finish(step, started):
        i, h = step
        lo, hi = ranges[i]
        rows = slice(i * QB, (i + 1) * QB)
        score, soft_grad, query, grad = started
        if h == 0:
            products[i] = jnp.transpose(
                mixed_grad[rows, lanes_o].astype(F32) * mixed[rows, lanes_o].astype(F32)
            )
        soft = jnp.exp(score - lse[pair, h : h + 1, rows])
        centre = jnp.sum(products[i][HEAD * h : HEAD * h + HEAD], axis=0, keepdims=True)
        score_grad = (soft * (soft_grad - centre)).astype(BF)
        soft = soft.astype(BF)
        return (
            mm(keys_t[HEAD * h : HEAD * h + HEAD, lo:hi], score_grad),
            mm(score_grad, query),
            mm(soft, grad),
        )

    current, done = start(steps[0]), {}
    for n, step in enumerate(steps):
        following = start(steps[n + 1]) if n + 1 < len(steps) else None
        done[step] = finish(step, current)
        current = following
        i, h = step
        if h == 1:
            (q0, k0, v0), (q1, k1, v1) = done.pop((i, 0)), done.pop((i, 1))
            rows = slice(i * QB, (i + 1) * QB)
            lo, hi = ranges[i]
            query_grad = jnp.transpose(jnp.concatenate([q0, q1], 0))
            qkv[rows, lanes_q] = (query_grad * HEAD**-0.5).astype(BF)
            keys, values, old = k0 + k1, v0 + v1, hi - QB - lo
            if old:
                key_acc[lo : lo + old] += keys[:old]
                value_acc[lo : lo + old] += values[:old]
            key_acc[hi - QB : hi] = keys[old:]
            value_acc[hi - QB : hi] = values[old:]
    qkv[:, lanes_k] = key_acc[...].astype(BF)
    qkv[:, lanes_v] = value_acc[...].astype(BF)


class Exchange:
    def __init__(self, mesh_shape, weights, shards, refs):
        self.depth = mesh_shape["fsdp"] // 2
        self.weights, self.shards = weights, shards
        self.__dict__.update(refs)
        dp, fsdp = lax.axis_index("dp"), lax.axis_index("fsdp")
        self.y, self.c = dp // 2, dp % 2
        self.z, self.x = fsdp // 2, fsdp % 2
        self.flips = [(b // 4, b // 2 % 2, b % 2) for b in range(1, 8)]

    def device(self, y=None, c=None, z=None, x=None):
        y, c = self.y if y is None else y, self.c if c is None else c
        z, x = self.z if z is None else z, self.x if x is None else x
        return (y * 2 + c, z * 2 + x)

    def far(self, d):
        return lax.rem(self.z + d, self.depth)

    def flipped(self, flip):
        own = (self.y, self.c, self.x)
        return [1 - a if f else a for a, f in zip(own, flip, strict=True)]

    def barrier(self):
        barrier = pltpu.get_barrier_semaphore()
        peers = [self.device(z=self.far(d)) for d in range(1, self.depth)]
        for flip in self.flips:
            y, c, x = self.flipped(flip)
            peers.append(self.device(y=y, c=c, x=x))
        for peer in peers:
            pl.semaphore_signal(barrier, inc=1, device_id=peer, device_id_type=MESH)
        pl.semaphore_wait(barrier, len(peers))

    def at(self, unit, y, c, z, x, lanes=slice(None)):
        return self.weights.at[unit, y, c, z, x, :, lanes]

    def remote(self, src, dst, sems, slot, device):
        return pltpu.make_async_remote_copy(
            src_ref=src,
            dst_ref=dst,
            send_sem=sems[0].at[slot],
            recv_sem=sems[1].at[slot],
            device_id=device,
            device_id_type=MESH,
        )

    def gather_copies(self, unit, step):
        y, c, z, x = self.y, self.c, self.z, self.x
        low, high, every = slice(0, HALF), slice(HALF, WIDTH), slice(None)
        to_x, to_y, to_c = self.device(x=1 - x), self.device(y=1 - y), self.device(c=1 - c)
        if step == 1:
            place = self.at(unit, y, c, z, x)
            moves = [(self.shards.at[unit], place, self.device(z=self.far(d))) for d in range(1, self.depth)]
        elif step == 2:
            one, two = [self.at(unit, y, c, every, x, lanes) for lanes in (low, high)]
            moves = [(one, one, to_x), (two, two, to_y)]
        elif step == 3:
            one = self.at(unit, y, c, every, every, low)
            two = self.at(unit, every, c, every, x, high)
            moves = [(one, one, to_y), (two, two, to_x)]
        else:
            core = self.at(unit, every, c, every, every)
            moves = [(core, core, to_c)]
        return [self.remote(src, dst, self.gather_sems, 4 * unit + step - 1, to) for src, dst, to in moves]

    def gather_all(self, unit, step):
        y, c, x, every = self.y, self.c, self.x, slice(None)
        part = (
            self.at(unit, y, c, slice(0, self.depth - 1), x),
            self.at(unit, y, c, every, x),
            self.at(unit, y, c, every, every),
            self.at(unit, every, c, every, every),
        )[step - 1]
        return self.remote(part, part, self.gather_sems, 4 * unit + step - 1, self.device(c=1 - c))

    def own_page(self, unit):
        place = self.at(unit, self.y, self.c, self.z, self.x)
        return pltpu.make_async_copy(self.shards.at[unit], place, self.local_sems.at[unit])

    def gather_step(self, unit, step):
        if step == 1:
            self.own_page(unit).start()
        if step == 2:
            self.own_page(unit).wait()
        if step > 1:
            self.gather_received(unit, step - 1)
        for copy in self.gather_copies(unit, step):
            copy.start()

    def gather_received(self, unit, step):
        self.gather_all(unit, step).wait_recv()

    def gather_sent(self, unit):
        for step in range(1, 5):
            self.gather_all(unit, step).wait_send()

    def vector_copies(self, step):
        y, c, z, x = self.y, self.c, self.z, self.x
        pages, landing = self.vec_pages, self.vec_landing
        moves = []
        if step == 1:
            place = pages.at[y, c, z, x]
            moves = [(self.vec_shard, place, self.device(z=self.far(d))) for d in range(1, self.depth)]
        elif step in (2, 3):
            for k, flip in enumerate(self.flips):
                yy, cc, xx = self.flipped(flip)
                own = pages.at[y, c, :, x]
                pair = (own, own) if step == 2 else (pages.at[yy, cc, :, xx], landing.at[k])
                moves.append((*pair, self.device(y=yy, c=cc, x=xx)))
        else:
            for d in range(1, self.depth):
                zz = self.far(d)
                moves.append((pages.at[y, c, zz, x], landing.at[7, d], self.device(z=zz)))
        return [self.remote(src, dst, self.vec_sems, step, to) for src, dst, to in moves]

    def vector_all(self, step):
        if step in (1, 4):
            part = self.vec_landing.at[7, 0 : self.depth - 1]
        else:
            part = self.vec_landing.at[0:7]
        return self.remote(part, part, self.vec_sems, step, self.device(c=1 - self.c))

    def vector_step(self, step):
        y, c, z, x = self.y, self.c, self.z, self.x
        pages, landing = self.vec_pages, self.vec_landing
        own = pltpu.make_async_copy(self.vec_shard, pages.at[y, c, z, x], self.local_sems.at[UNITS])
        if step == 1:
            own.start()
        elif step == 2:
            own.wait()
        if step in (2, 4, 5):
            self.vector_all(step - 1).wait_recv()
        if step == 4:
            for k in range(self.depth):
                total = pages[y, c, k, x]
                for j in range(7):
                    total = total + landing[j, k]
                pages[y, c, k, x] = total
        if step == 5:
            total = pages[y, c, z, x]
            for d in range(1, self.depth):
                total = total + landing[7, d]
            self.vec_sum[...] = total
            return
        for copy in self.vector_copies(step):
            copy.start()

    def vectors_sent(self, *steps):
        for step in steps:
            self.vector_all(step).wait_send()

    def add(self, place, other):
        place[...] = (place[...].astype(F32) + other[...].astype(F32)).astype(BF)

    def sum_copies(self, unit, slot, step):
        y, c, z, x = self.y, self.c, self.z, self.x
        low, high, every = slice(0, HALF), slice(HALF, WIDTH), slice(None)
        to_x, to_y, to_c = self.device(x=1 - x), self.device(y=1 - y), self.device(c=1 - c)
        if step == 1:
            moves = [(self.at(slot, every, 1 - c, every, every), self.from_core.at[unit], to_c)]
        elif step == 2:
            two = self.from_two
            moves = [(self.at(slot, 1 - y, c, every, every, low), two.at[unit, 0], to_y)]
            for k in range(2):
                moves.append((self.at(slot, k, c, every, 1 - x, high), two.at[unit, 1, :, k], to_x))
        elif step == 3:
            three = self.from_three
            moves = [
                (self.at(slot, y, c, every, 1 - x, low), three.at[unit, 0], to_x),
                (self.at(slot, 1 - y, c, every, x, high), three.at[unit, 1], to_y),
            ]
        else:
            moves = []
            for d in range(1, self.depth):
                zz = self.far(d)
                moves.append((self.at(slot, y, c, zz, x), self.from_four.at[unit, d - 1], self.device(z=zz)))
        return [self.remote(src, dst, self.sum_sems, 4 * unit + step - 1, to) for src, dst, to in moves]

    def sum_all(self, unit, slot, step):
        y, c, x, every = self.y, self.c, self.x, slice(None)
        src, dst = (
            (self.at(slot, every, c, every, every), self.from_core.at[unit]),
            (self.at(slot, y, c, every, every), self.from_two.at[unit]),
            (self.at(slot, y, c, every, x), self.from_three.at[unit]),
            (self.at(slot, y, c, slice(0, self.depth - 1), x), self.from_four.at[unit]),
        )[step - 1]
        return self.remote(src, dst, self.sum_sems, 4 * unit + step - 1, self.device(c=1 - c))

    def sum_sent(self, unit, slot):
        for step in range(1, 5):
            self.sum_all(unit, slot, step).wait_send()

    def sum_step(self, unit, slot, step):
        y, c, z, x = self.y, self.c, self.z, self.x
        low, high = slice(0, HALF), slice(HALF, WIDTH)
        if step > 1:
            self.sum_all(unit, slot, step - 1).wait_recv()
        def add_one(k, carry):
            if step == 2:
                for j in range(2):
                    for i in range(2):
                        self.add(self.at(slot, j, c, k, i), self.from_core.at[unit, j, k, i])
            elif step == 3:
                for j in range(2):
                    self.add(self.at(slot, y, c, k, j, low), self.from_two.at[unit, 0, k, j])
                    self.add(self.at(slot, j, c, k, x, high), self.from_two.at[unit, 1, k, j])
            else:
                self.add(self.at(slot, y, c, k, x, low), self.from_three.at[unit, 0, k])
                self.add(self.at(slot, y, c, k, x, high), self.from_three.at[unit, 1, k])
            return carry

        if step > 1:
            lax.fori_loop(0, self.depth, add_one, 0)
        for copy in self.sum_copies(unit, slot, step):
            copy.start()

    def summed(self, unit, slot):
        self.sum_all(unit, slot, 4).wait_recv()
        total = self.at(slot, self.y, self.c, self.z, self.x)[...].astype(F32)
        for d in range(self.depth - 1):
            total += self.from_four[unit, d].astype(F32)
        return total


def block_kernel(mesh_shape, exchanged, *refs):
    refs = list(refs)
    take = lambda n: [refs.pop(0) for _ in range(n)]
    tokens, cotangent, documents = take(3)
    if exchanged:
        shards, vec_shard = take(2)
    else:
        weights_in, vectors_in = take(2)
    result, input_grad = take(2)
    if exchanged:
        qkv_sum, out_sum, up_sum, down_sum, vec_sum = take(5)
    else:
        weights_out, vectors_out = take(2)
    (weights, cot, normed_one, qkv, mixed, lse, masks, residual, normed_two) = take(9)
    (acc_one, acc_two, low_one, low_two, fvec, svec, io_sems) = take(7)
    x_in = low_two
    key_acc, value_acc = residual.at[:, 0:128], residual.at[:, 128:256]
    length = x_in.shape[0]
    tiles = length // QB

    ex = None
    if exchanged:
        names = ("vec_pages", "vec_landing", "from_core", "from_two", "from_three", "from_four")
        extra = dict(zip(names, take(len(names))))
        gs, gr, ss, sr, vs, vr, local = take(7)
        extra.update(gather_sems=(gs, gr), sum_sems=(ss, sr), vec_sems=(vs, vr), local_sems=local)
        extra.update(vec_shard=vec_shard, vec_sum=vec_sum)
        ex = Exchange(mesh_shape, weights, shards, extra)

    def matrix(unit, start=0, width=WIDTH):
        lanes = pl.ds(start, width)
        if exchanged:
            return weights[unit, :, :, :, :, :, lanes].reshape(WIDTH, width)
        return weights[unit, :, lanes]

    def matrix_rows(unit, half):
        if exchanged:
            return weights[unit, half].reshape(HALF, WIDTH)
        return weights[unit, pl.ds(pl.multiple_of(HALF * half, HALF), HALF)]

    def gradient(unit, left, right):
        def step(half, carry):
            lanes = pl.ds(pl.multiple_of(HALF * half, 128), HALF)
            values = dg(left[:, lanes], right(), 0, 0).astype(BF)
            if exchanged:
                weights[unit, half] = values.reshape(weights.shape[2:])
            else:
                weights[unit, lanes] = values
            return carry

        lax.fori_loop(0, 2, step, 0)

    def tile_loop(body, size=QB):
        def step(i, carry):
            body(pl.ds(pl.multiple_of(i * size, size), size))
            return carry

        lax.fori_loop(0, length // size, step, 0)

    def fv(row, size=1):
        return fvec[row : row + 1, 0 : WIDTH * size]

    def tokens_sum(values):
        return jnp.sum(values.astype(F32), axis=0, keepdims=True)

    def copy(slot):
        src, dst = ((tokens, x_in), (cotangent, cot), (acc_one, result), (acc_two, input_grad))[slot]
        return pltpu.make_async_copy(src, dst, io_sems.at[slot])

    def place(name, turn=0):
        for index, steps in SCHEDULE.get(name, {}).items() if exchanged else ():

            def run(steps=steps):
                for of_sum, unit, step in steps:
                    if of_sum:
                        add_up(unit, step)
                    else:
                        ex.gather_step(unit, step)

            if isinstance(turn, int):
                if turn == index:
                    run()
            else:
                pl.when(turn == index)(run)

    def begin(unit, slot=None):
        if exchanged:
            ex.sum_step(unit, unit if slot is None else slot, 1)

    def arrived(unit):
        if exchanged:
            ex.gather_received(unit, 4)

    def add_up(unit, step):
        slot = up(unit) if unit < OUT else unit
        if step < 5:
            ex.sum_step(unit, slot, step)
            return
        total = ex.summed(unit, slot)
        rows = total.shape[0]
        chunk, kind = (unit - up(0)) // 2, (unit - up(0)) % 2
        if unit < OUT:
            for part in range(3):
                start = WIDTH * part + 256 * unit
                qkv_sum[:, start : start + 256] = total[:, 256 * part : 256 * part + 256]
        elif unit == OUT:
            out_sum[...] = total
        elif kind == 0:
            up_sum[chunk] = total
        else:
            down_sum[rows * chunk : rows * chunk + rows] = total

    copy(0).start()
    copy(1).start()
    svec[...] = jnp.zeros(svec.shape, F32)
    if exchanged:
        ex.barrier()
        ex.vector_step(1)
        for unit in range(UNITS):
            ex.gather_step(unit, 1)
        build_masks(documents, masks, False)
        place("masks")
        ex.vector_step(2)
        place("vec")
        ex.vector_all(2).wait_recv()
        ex.vectors_sent(1, 2)
        pages_to_rows(ex.vec_pages.reshape(32, VEC_ROWS, 128), fvec, 32)
        place("rows")
    else:
        weights_copy = pltpu.make_async_copy(weights_in, weights, io_sems.at[4])
        weights_copy.start()
        build_masks(documents, masks, False)
        fvec[...] = vectors_in[...]
    copy(0).wait()

    def norm_one(rows):
        normed, _ = norm_stats(x_in[rows].astype(F32))
        normed_one[rows] = (normed * fv(0) + fv(1)).astype(BF)

    tile_loop(norm_one)
    place("norm")
    if not exchanged:
        weights_copy.wait()

    def attention(unit, carry):
        place("att0", unit)
        arrived(unit)
        bias_lanes = [pl.ds(pl.multiple_of(WIDTH * k + 256 * unit, 256), 256) for k in range(2)]
        lanes = [pl.ds(pl.multiple_of(WIDTH * unit + 256 * k, 256), 256) for k in range(3)]

        def project(rows):
            full = mm(normed_one[rows], matrix(unit))
            query = (full[:, 0:256] + fvec[2:3, bias_lanes[0]]).astype(BF).astype(F32)
            qkv[rows, lanes[0]] = (query * HEAD**-0.5).astype(BF)
            qkv[rows, lanes[1]] = full[:, 256:512].astype(BF)
            qkv[rows, lanes[2]] = (full[:, 512:] + fvec[2:3, bias_lanes[1]]).astype(BF)

        tile_loop(project, 2 * QB)
        place("att1", unit)

        def pair(half, carry):
            forward_pair(unit, half, qkv, mixed, lse, masks)
            place("att2", 2 * unit + half)
            return carry

        return lax.fori_loop(0, 2, pair, carry)

    lax.fori_loop(0, 3, attention, 0)

    place("attend")
    arrived(OUT)
    copy(1).wait()

    def attend(rows):
        total = x_in[rows].astype(F32) + (mm(mixed[rows], matrix(OUT)) + fv(3))
        residual[rows] = total
        normed, _ = norm_stats(total)
        normed_two[rows] = (normed * fv(4) + fv(5)).astype(BF)
        acc_one[rows] = total + fv(7)
        acc_two[rows] = jnp.zeros_like(total)

    tile_loop(attend)
    place("attended")
    build_masks(documents, masks, True)
    place("masksT")

    def feed_forward(chunk, carry):
        up_unit, down_unit = up(chunk), down(chunk)
        place("ff0", chunk)
        arrived(up_unit)
        arrived(down_unit)

        def half_hidden(half, carry):
            lanes = pl.ds(pl.multiple_of(HALF * half, 128), HALF)
            wide = pl.ds(pl.multiple_of(WIDTH * chunk + HALF * half, 128), HALF)

            def hidden(start):
                rows = slice(start, start + QB)
                pre = mm(normed_two[rows], matrix(up_unit, lanes.start, HALF)) + fvec[6:7, wide]
                return pre, dg(cot[rows], matrix_rows(down_unit, half), 1, 1)

            def activate(start, pair):
                pre, grad = pair
                square = pre * pre
                bent = jnp.tanh(pre * (GELU_COEF + (GELU_COEF * GELU_CUBIC) * square))
                upper = 0.5 + 0.5 * bent
                slope = upper + (0.5 * pre) * (1.0 - bent * bent) * (
                    GELU_COEF + (3.0 * GELU_COEF * GELU_CUBIC) * square
                )
                rows = slice(start, start + QB)
                low_one[rows, lanes] = (pre * upper).astype(BF)
                back = (grad * slope).astype(BF)
                low_two[rows, lanes] = back
                svec[6:7, wide] += tokens_sum(back)

            current = hidden(0)
            for i in range(tiles):
                following = hidden((i + 1) * QB) if i + 1 < tiles else None
                activate(i * QB, current)
                current = following
            place("ff1", 2 * chunk + half)
            return carry

        lax.fori_loop(0, 2, half_hidden, 0)

        def outward(rows):
            acc_one[rows] += mm(low_one[rows], matrix(down_unit))
            acc_two[rows] += dg(low_two[rows], matrix(up_unit), 1, 1)

        tile_loop(outward, 2 * QB)
        place("ff3", chunk)
        if exchanged:
            ex.gather_sent(down_unit)
        gradient(down_unit, low_one, lambda: cot[...])
        begin(down_unit)
        place("ff4", chunk)
        if exchanged:
            ex.gather_sent(up_unit)
        gradient(up_unit, normed_two, lambda: low_two[...])
        begin(up_unit)
        place("ff5", chunk)
        return carry

    lax.fori_loop(0, 4, feed_forward, 0)
    copy(2).start()

    def back_two(rows):
        normed, scale = norm_stats(residual[rows])
        grad = acc_two[rows]
        grads = cot[rows].astype(F32)
        total = grads + norm_back(grad, fv(4), normed, scale)
        acc_two[rows] = total
        low = total.astype(BF)
        low_two[rows] = low
        for row, part in ((4, grad * normed), (5, grad), (7, grads), (3, low)):
            svec[row : row + 1, 0:WIDTH] += tokens_sum(part)

    def back_out(rows):
        low_one[rows] = dg(low_two[rows], matrix(OUT), 1, 1).astype(BF)

    tile_loop(back_two)
    place("back_two")
    tile_loop(back_out, 2 * QB)
    place("back_out")
    if exchanged:
        ex.gather_sent(OUT)
    gradient(OUT, mixed, lambda: low_two[...])
    begin(OUT)
    place("dWo")
    copy(2).wait()
    copy(0).start()

    def attention_back(unit, carry):
        slot = up(unit)

        def pair(half, carry):
            backward_pair(unit, half, qkv, mixed, low_one, lse, masks, key_acc, value_acc)

            place("ab0", 2 * unit + half)
            return carry

        lax.fori_loop(0, 2, pair, 0)
        all_three = pl.ds(pl.multiple_of(WIDTH * unit, WIDTH), WIDTH)
        if exchanged:
            ex.sum_sent(slot, slot)
        else:
            done = pltpu.make_async_copy(weights.at[slot], weights_out.at[slot], io_sems.at[4])
            done.start()
            done.wait()
        gradient(slot, normed_one, lambda: qkv[:, all_three])
        begin(unit, slot)
        place("ab2", unit)
        for part, row in ((0, 0), (2, WIDTH)):
            lanes = pl.ds(pl.multiple_of(WIDTH * unit + 256 * part, 256), 256)
            bias = pl.ds(pl.multiple_of(row + 256 * unit, 256), 256)
            svec[2:3, bias] = tokens_sum(qkv[:, lanes])

        return carry

    def back_qkv(rows):
        total = dg(qkv[rows, 0:WIDTH], matrix(0), 1, 1)
        for unit in (1, 2):
            total += dg(qkv[rows, WIDTH * unit : WIDTH * unit + WIDTH], matrix(unit), 1, 1)
        acc_one[rows] = total
        place("da1", rows.start // (2 * QB))

    lax.fori_loop(0, 3, attention_back, 0)
    tile_loop(back_qkv, 2 * QB)
    copy(0).wait()

    def back_one(rows):
        normed, scale = norm_stats(x_in[rows].astype(F32))
        grad = acc_one[rows]
        acc_two[rows] += norm_back(grad, fv(0), normed, scale)
        for row, part in ((0, grad * normed), (1, grad)):
            svec[row : row + 1, 0:WIDTH] += tokens_sum(part)

    tile_loop(back_one)
    copy(3).start()
    if exchanged:
        place("back_one")
        rows_to_pages(svec, ex.vec_pages.reshape(32, VEC_ROWS, 128), 32)
        ex.vector_step(3)
        place("r2p")
        ex.vector_step(4)
        place("drain")
        ex.vector_step(5)
        ex.vectors_sent(3, 4)
        for unit in range(3):
            ex.gather_sent(unit)
            ex.sum_sent(unit, up(unit))
        for unit in (OUT, up(3), *map(down, range(4))):
            ex.sum_sent(unit, unit)
    else:
        vectors_out[...] = svec[...]
        own = [(k, k) for k in (OUT, up(3), *map(down, range(4)))]
        for src, dst in [(up(k), k) for k in range(3)] + own:
            done = pltpu.make_async_copy(weights.at[src], weights_out.at[dst], io_sems.at[4])
            done.start()
            done.wait()
    copy(3).wait()


def finish_kernel(*refs):
    page, outs = refs[6], refs[7:]
    outs[0][...] = refs[0][...]
    outs[1][...] = refs[1][...]

    @pl.when(pl.program_id(0) == 0)
    def _():
        for k in (2, 3, 5):
            outs[k][...] = refs[k][...]
        up, rows = refs[4], refs[4].shape[1]
        shards = WIDTH // rows
        groups = [
            jnp.concatenate([up[j, :, 4 * rows * g : 4 * rows * g + 4 * rows] for j in range(4)], 1)
            for g in range(shards // 4)
        ]
        moved = lax.dot_general(
            jnp.concatenate(groups, 0),
            regroup(rows, True).astype(F32),
            (((1,), (0,)), ((), ())),
            preferred_element_type=F32,
            precision=lax.Precision.HIGHEST,
        )
        for g in range(shards // 4):
            outs[4][:, HALF * g : HALF * g + HALF] = moved[rows * g : rows * g + rows]
        for r, dst in enumerate(outs[6:]):
            dst[...] = page[r, 0 : dst.shape[0]]


def finish(rows, sums, page, sizes):
    block = pl.BlockSpec((rows[0].shape[0] // 2, WIDTH), lambda i: (i, 0))
    whole = lambda shape: pl.BlockSpec(shape, lambda i: (0,) * len(shape))
    ins = [block, block] + [whole(a.shape) for a in (*sums, page)]
    qkv, out, up, down = [a.shape for a in sums]
    shapes = [qkv, out, (up[1], 4 * WIDTH), down] + [(n,) for n in sizes]
    outs = [block, block] + [whole(shape) for shape in shapes]
    shapes = [a.shape for a in rows] + shapes
    return pl.pallas_call(
        finish_kernel,
        grid=(2,),
        in_specs=ins,
        out_specs=outs,
        out_shape=[jax.ShapeDtypeStruct(shape, F32) for shape in shapes],
        name="finish",
    )(*rows, *sums, page)


def run_block(mesh_shape, exchanged, tokens, cotangent, documents, *weights):
    length, width = tokens.shape
    depth = mesh_shape["fsdp"] // 2
    vmem = pltpu.VMEM
    whole = pl.BlockSpec(memory_space=pltpu.VMEM)
    far = pl.BlockSpec(memory_space=pl.ANY)
    blocks = len(mask_blocks(length))
    rows = [jax.ShapeDtypeStruct((length, WIDTH), F32)] * 2
    if exchanged:
        shard = weights[0].shape[1]
        in_specs = [far, far, whole, far, far]
        out_shape = rows + [
            jax.ShapeDtypeStruct((shard, 3 * WIDTH), F32),
            jax.ShapeDtypeStruct((shard, WIDTH), F32),
            jax.ShapeDtypeStruct((4, shard, WIDTH), F32),
            jax.ShapeDtypeStruct((4 * shard, WIDTH), F32),
            jax.ShapeDtypeStruct((VEC_ROWS, 128), F32),
        ]
        out_specs = [far, far] + [whole] * 5
        places = (2, 2, depth, 2)
        held = [vmem((UNITS, *places, shard, WIDTH), BF)]
    else:
        in_specs = [far, far, whole, far, whole]
        out_shape = rows + [
            jax.ShapeDtypeStruct((UNITS, WIDTH, WIDTH), BF),
            jax.ShapeDtypeStruct((VEC_ROWS, 4 * WIDTH), F32),
        ]
        out_specs = [far, far, far, whole]
        held = [vmem((UNITS, WIDTH, WIDTH), BF)]
    low, full = vmem((length, WIDTH), BF), vmem((length, WIDTH), F32)
    scratch = held + [
        low,
        low,
        vmem((length, 3 * WIDTH), BF),
        low,
        vmem((6, 8, length), F32),
        vmem((blocks, QB, QB), F32),
        full,
        low,
        full,
        full,
        low,
        low,
        vmem((VEC_ROWS, 4 * WIDTH), F32),
        vmem((VEC_ROWS, 4 * WIDTH), F32),
        pltpu.SemaphoreType.DMA((8,)),
    ]
    if exchanged:
        dma = pltpu.SemaphoreType.DMA
        scratch += [
            vmem((2, 2, depth, 2, VEC_ROWS, 128), F32),
            vmem((8, depth, VEC_ROWS, 128), F32),
            vmem((UNITS, 2, depth, 2, shard, WIDTH), BF),
            vmem((UNITS, 2, depth, 2, shard, HALF), BF),
            vmem((UNITS, 2, depth, shard, HALF), BF),
            vmem((UNITS, depth - 1, shard, WIDTH), BF),
            dma((4 * UNITS,)),
            dma((4 * UNITS,)),
            dma((4 * UNITS,)),
            dma((4 * UNITS,)),
            dma((5,)),
            dma((5,)),
            dma((UNITS + 1,)),
        ]
    params = dict(vmem_limit_bytes=VMEM_BYTES)
    if exchanged:
        params.update(collective_id=0, has_side_effects=True)
    return pl.pallas_call(
        functools.partial(block_kernel, mesh_shape, exchanged),
        out_shape=out_shape,
        in_specs=in_specs,
        out_specs=out_specs,
        scratch_shapes=scratch,
        compiler_params=pltpu.CompilerParams(**params),
        name="block",
    )(tokens, cotangent, documents, *weights)


def local(mesh_shape, tokens, cotangent, document_ids, source_layer, *stacks):
    (attngain, attnshift, qkvmatrix, qvoffset, outmatrix, outoffset) = stacks[:6]
    (mlpgain, mlpshift, upmatrix, upoffset, downmatrix, downoffset) = stacks[6:]
    vectors = (attngain, attnshift, qvoffset, outoffset, mlpgain, mlpshift, upoffset, downoffset)
    matrices = (qkvmatrix, outmatrix, upmatrix, downmatrix)
    rows_seq, length, width = tokens.shape
    shard = qkvmatrix.shape[1]
    shards = WIDTH // shard
    x_rows, c_rows = tokens.reshape(length, width), cotangent.reshape(length, width)
    axes = ("dp", "fsdp")
    exchanged = mesh_shape["dp"] == 4 and mesh_shape["fsdp"] == 8 and shard % 8 == 0
    if exchanged:
        units, page = pack_layer(source_layer, vectors, matrices)
        result, input_grad, qkv, out, wide, tall, page = run_block(
            mesh_shape, True, x_rows, c_rows, document_ids, units, page
        )
        result, input_grad, qkv, out, wide, tall, *pieces = finish(
            (result, input_grad), (qkv, out, wide, tall), page, [shard * s for s in VEC_SIZES]
        )
    else:
        pick = lambda stack: lax.dynamic_index_in_dim(stack, source_layer, 0, keepdims=False)
        gather = lambda part: lax.all_gather(part, axes, axis=0, tiled=True)
        scatter = lambda part: lax.psum_scatter(part, axes, scatter_dimension=0, tiled=True)
        qkv, out, wide, tall = [gather(pick(m)) for m in matrices]
        thirds = qkv.reshape(WIDTH, 3, 3, 256).transpose(2, 0, 1, 3).reshape(3, WIDTH, WIDTH)
        ups, downs = wide.reshape(WIDTH, 4, WIDTH).transpose(1, 0, 2), tall.reshape(4, WIDTH, WIDTH)
        quarters = jnp.stack([ups, downs], 1).reshape(8, WIDTH, WIDTH)
        weights = jnp.concatenate([thirds, out[None], quarters], 0)
        rows = [gather(pick(v)).astype(F32) for v in vectors]
        table = jnp.stack([jnp.pad(r, (0, 4 * WIDTH - r.shape[0])) for r in rows])
        result, input_grad, weights, table = run_block(
            mesh_shape, False, x_rows, c_rows, document_ids, weights, table
        )
        weights = weights.astype(F32)
        qkv = weights[0:3].reshape(3, WIDTH, 3, 256).transpose(1, 2, 0, 3).reshape(WIDTH, -1)
        wide = weights[up(0) :: 2].transpose(1, 0, 2).reshape(WIDTH, -1)
        tall = weights[down(0) :: 2].reshape(4 * WIDTH, WIDTH)
        qkv, out, wide, tall = [scatter(m) for m in (qkv, weights[OUT], wide, tall)]
        pieces = [scatter(table[r, 0 : WIDTH * s]) for r, s in enumerate(VEC_SIZES)]
    gain, shift, qv, outb, mid_gain, mid_shift, upb, downb = pieces
    shape = tokens.shape
    return (
        result.reshape(shape),
        input_grad.reshape(shape),
        gain,
        shift,
        qkv,
        qv,
        out,
        outb,
        mid_gain,
        mid_shift,
        wide,
        upb,
        tall,
        downb,
    )


def solution(mesh):
    axes = ("dp", "fsdp")
    rows, vector, matrix = P(axes, None, None), P(None, axes), P(None, axes, None)
    return jax.shard_map(
        functools.partial(local, dict(mesh.shape)),
        mesh=mesh,
        in_specs=(
            rows,
            rows,
            P(axes, None),
            P(),
            vector,
            vector,
            matrix,
            vector,
            matrix,
            vector,
            vector,
            vector,
            matrix,
            vector,
            matrix,
            vector,
        ),
        out_specs=(
            rows,
            rows,
            P(axes),
            P(axes),
            P(axes, None),
            P(axes),
            P(axes, None),
            P(axes),
            P(axes),
            P(axes),
            P(axes, None),
            P(axes),
            P(axes, None),
            P(axes),
        ),
        check_vma=False,
    )
```

profile of v0, /device:TPU:0, one launch (start us, length us, event | category | flops | bytes accessed | tf_op | source)
XLA Modules:
  0.0 169.4 jit_solution(9792286539071717988)
XLA Ops:
  1.3 2.3 %pick_layer.1 = (bf16[12,24,768]{2,1,0:T(8,128)(2,1)}, f32[8,128]{1,0:T(8,128)}) custom-call(s32[1]{0:T(128)} %bitcast.5.layer_ref, bf16[12,24]{1,0:T(8,128)(2,1)} %refs_0_.1, bf16[12,24]{1,0:T(8,128)(2,1)} %refs_1_.1, bf16[12,48]{1,0:T(8,128)(2,1)} %refs_2_.2, bf16[12,24]{1,0:T(8,128)(2,1)} %refs_3_.1, bf16[12,24]{1,0:T(8,128)(2,1)} %refs_4_.1, ...), custom_call_target="tpu_custom_call" | custom-call | tf_op jit(solution)/shard_map/pick_layer/pallas_call | solution.py:178
  3.6 159.5 %block.1 = (f32[1024,768]{1,0:T(8,128)}, f32[1024,768]{1,0:T(8,128)}, f32[24,2304]{1,0:T(8,128)}, f32[24,768]{1,0:T(8,128)}, f32[4,24,768]{2,1,0:T(8,128)}, /*index=5*/f32[96,768]{1,0:T(8,128)}, f32[8,128]{1,0:T(8,128)}) custom-call(bf16[1024,768]{1,0:T(8,128)(2,1)} %bitcast.6, bf16[1024,768]{1,0:T(8,128)(2,1)} %bitcast.7, s32[1,1024]{1,0:T(1,128)} %refs_2_.3, ...), custom_call_target="tpu_custom_call" | custom-call | tf_op jit(solution)/shard_map/block/pallas_call | solution.py:1080
  163.1 6.2 %finish.1 = (f32[1024,768]{1,0:T(8,128)}, f32[1024,768]{1,0:T(8,128)}, f32[24,2304]{1,0:T(8,128)}, f32[24,768]{1,0:T(8,128)}, f32[24,3072]{1,0:T(8,128)}, /*inde...) custom-call(f32[1024,768]{1,0:T(8,128)} %get-tuple-element.39.refs_0, ...), custom_call_target="tpu_custom_call" | custom-call | tf_op jit(solution)/shard_map/finish/pallas_call | solution.py:1003
where the time goes:
time: 170 us; the launch traced here: 169 us
  Pallas kernels  168 us (99%)
    pallas_call x1, Pallas kernels, run_block(): pl.pallas_call(functools.partial(block_kernel, mesh_shape, exchanged), ou...  159 us
    pallas_call x1, Pallas kernels, finish(): pl.pallas_call(finish_kernel, grid=(2,), in_specs=ins, out_specs=outs, ou...  6.18 us

commit v1 on v0

--- a/solution.py
+++ b/solution.py
@@ -22,6 +22,8 @@
 VMEM_BYTES = 63 * 2**20
 VEC_SIZES = (1, 1, 2, 1, 1, 1, 4, 1)
 OUT, UNITS = 3, 12
+TURNED = (6, 10)
+LAST, LAST_HALF = 2, 12
 
 
 def up(quarter):
@@ -37,84 +39,89 @@
         0: ((0, 0, 2),),
     },
     "att0": {
-        0: ((0, 1, 2), (0, 0, 3), (0, 2, 2), (0, 1, 3), (0, 3, 2), (0, 0, 4), (0, 2, 3),),
+        0: ((0, 1, 2), (0, 0, 3), (0, 2, 2), (0, 1, 3), (0, 3, 2), (0, 0, 4), (0, 2, 3), (0, 6, 2),),
+    },
+    "att1": {
+        0: ((0, 4, 2),),
     },
     "att2": {
-        0: ((0, 4, 2),),
-        1: ((0, 1, 4), (0, 3, 3), (0, 5, 2),),
-        2: ((0, 4, 3),),
-        3: ((0, 7, 2),),
-        4: ((0, 5, 3), (0, 6, 3), (0, 8, 2),),
-        5: ((0, 9, 2),),
-    },
-    "att1": {
-        1: ((0, 2, 4), (0, 6, 2),),
-        2: ((0, 3, 4),),
+        0: ((0, 1, 4),),
+        1: ((0, 3, 3), (0, 5, 2),),
+        2: ((0, 2, 4), (0, 6, 3), (0, 7, 2),),
+        3: ((0, 4, 3), (0, 8, 2),),
+        4: ((0, 3, 4),),
+        5: ((0, 5, 3), (0, 7, 3), (0, 9, 2), (0, 10, 2),),
     },
     "attended": {
-        0: ((0, 4, 4), (0, 10, 2),),
+        0: ((0, 11, 2),),
     },
     "masksT": {
-        0: ((0, 7, 3),),
+        0: ((0, 4, 4),),
     },
     "ff0": {
-        0: ((0, 11, 2), (0, 5, 4),),
-        1: ((0, 7, 4), (1, 5, 2), (0, 11, 3), (1, 4, 2),),
+        0: ((0, 8, 3), (0, 5, 4),),
     },
     "ff1": {
-        1: ((0, 6, 4),),
-        3: ((0, 8, 4),),
-        4: ((1, 7, 2), (1, 5, 3),),
-        5: ((1, 6, 2),),
-        6: ((1, 7, 3), (1, 5, 4), (1, 9, 2),),
-        7: ((1, 8, 2),),
+        0: ((0, 7, 4),),
+        1: ((0, 9, 3),),
+        2: ((0, 8, 4), (1, 5, 2), (1, 4, 2),),
+        3: ((0, 9, 4),),
+        4: ((1, 5, 3), (1, 7, 2),),
+        5: ((0, 10, 4), (1, 4, 3), (1, 6, 2),),
+        6: ((1, 4, 4), (1, 9, 2), (1, 8, 2), (1, 5, 5),),
+        7: ((1, 6, 3),),
     },
     "ff3": {
-        0: ((0, 8, 3), (0, 9, 3),),
-        1: ((0, 9, 4),),
-        2: ((0, 11, 4),),
-        3: ((1, 4, 4), (1, 6, 3),),
+        0: ((0, 6, 4), (0, 10, 3),),
+        2: ((1, 5, 4),),
+        3: ((1, 7, 4),),
     },
     "ff4": {
-        0: ((0, 10, 3),),
-        2: ((1, 4, 3),),
-        3: ((1, 7, 4), (1, 5, 5),),
+        0: ((0, 11, 3),),
+        1: ((0, 11, 4),),
+        3: ((1, 4, 5),),
     },
     "ff5": {
-        1: ((0, 10, 4),),
+        2: ((1, 7, 3),),
         3: ((1, 9, 3),),
     },
     "back_two": {
-        0: ((1, 11, 2), (1, 8, 3), (1, 10, 2), (1, 4, 5),),
+        0: ((1, 8, 3), (1, 11, 2), (1, 6, 4), (1, 10, 2), (1, 7, 5),),
     },
     "back_out": {
-        0: ((1, 6, 4), (1, 7, 5),),
+        0: ((1, 9, 4),),
     },
     "dWo": {
-        0: ((1, 9, 4),),
+        0: ((1, 8, 4),),
     },
     "ab0": {
-        0: ((1, 11, 3), (1, 3, 2), (1, 8, 4),),
-        1: ((1, 10, 3), (1, 6, 5), (1, 9, 5),),
-        2: ((1, 3, 3), (1, 0, 2), (1, 8, 5),),
-        3: ((1, 10, 4), (1, 11, 5),),
+        0: ((1, 11, 3), (1, 3, 2), (1, 6, 5),),
+        1: ((1, 10, 3), (1, 9, 5),),
+        2: ((1, 10, 4), (1, 3, 3), (1, 0, 2),),
+        3: ((1, 11, 5),),
         4: ((1, 0, 3), (1, 1, 2),),
-        5: ((1, 10, 5),),
+        5: ((1, 0, 4), (1, 2, 2), (1, 3, 5),),
     },
     "ab2": {
-        0: ((1, 11, 4),),
-        1: ((1, 3, 4),),
-        2: ((1, 0, 4), (1, 3, 5),),
+        0: ((1, 11, 4), (1, 8, 5),),
+        1: ((1, 3, 4), (1, 10, 5),),
     },
     "da1": {
-        0: ((1, 1, 3),),
-        1: ((1, 2, 2),),
+        0: ((1, 1, 3), (1, 12, 2), (1, 2, 3),),
+        1: ((1, 0, 5),),
     },
     "back_one": {
-        0: ((1, 1, 4), (1, 0, 5),),
+        0: ((1, 1, 4),),
+    },
+    "r2p": {
+        0: ((1, 12, 3), (1, 2, 4),),
+    },
+    "y": {
+        0: ((1, 12, 4),),
+        1: ((1, 1, 5), (1, 2, 5),),
     },
     "drain": {
-        0: ((1, 2, 3), (1, 1, 5), (1, 2, 4), (1, 2, 5),),
+        0: ((1, 12, 5),),
     },
 }
 
@@ -145,9 +152,10 @@
     layer = layer_ref[0]
     for t in range(3):
         for part in range(3):
-            units[t, :, 256 * part : 256 * part + 256] = qkv[
-                0, :, WIDTH * part + 256 * t : WIDTH * part + 256 * t + 256
-            ]
+            for half in range(2):
+                start = WIDTH * part + 256 * t + 128 * half
+                lanes = slice(HALF * half + 128 * part, HALF * half + 128 * part + 128)
+                units[t, :, lanes] = qkv[0, :, start : start + 128]
     units[OUT] = out[0]
     rows = units.shape[1]
     shards = WIDTH // rows
@@ -293,7 +301,7 @@
 
 
 def pair_lanes(unit, half):
-    start = [unit * WIDTH + 256 * part + 128 * half for part in range(3)]
+    start = [unit * WIDTH + HALF * half + 128 * part for part in range(3)]
     return [pl.ds(pl.multiple_of(s, 128), 128) for s in start]
 
 
@@ -398,6 +406,10 @@
     qkv[:, lanes_v] = value_acc[...].astype(BF)
 
 
+def turned(unit):
+    return isinstance(unit, int) and unit in TURNED
+
+
 class Exchange:
     def __init__(self, mesh_shape, weights, shards, refs):
         self.depth = mesh_shape["fsdp"] // 2
@@ -447,7 +459,9 @@
         y, c, z, x = self.y, self.c, self.z, self.x
         low, high, every = slice(0, HALF), slice(HALF, WIDTH), slice(None)
         to_x, to_y, to_c = self.device(x=1 - x), self.device(y=1 - y), self.device(c=1 - c)
-        if step == 1:
+        if turned(unit) and step < 4:
+            moves = self.turned_moves(unit, step)
+        elif step == 1:
             place = self.at(unit, y, c, z, x)
             moves = [(self.shards.at[unit], place, self.device(z=self.far(d))) for d in range(1, self.depth)]
         elif step == 2:
@@ -462,9 +476,29 @@
             moves = [(core, core, to_c)]
         return [self.remote(src, dst, self.gather_sems, 4 * unit + step - 1, to) for src, dst, to in moves]
 
+    def turned_moves(self, unit, step):
+        y, c, z, x = self.y, self.c, self.z, self.x
+        low, high, every = slice(0, HALF), slice(HALF, WIDTH), slice(None)
+        to_x, to_y = self.device(x=1 - x), self.device(y=1 - y)
+        if step == 1:
+            return [
+                (self.shards.at[unit, :, lanes], self.at(unit, y, c, z, x, lanes), to)
+                for lanes, to in ((low, to_x), (high, to_y))
+            ]
+        if step == 2:
+            one, two = self.at(unit, y, c, z, every, low), self.at(unit, every, c, z, x, high)
+            return [(one, one, to_y), (two, two, to_x)]
+        plane = self.at(unit, every, c, z, every)
+        return [(plane, plane, self.device(z=self.far(d))) for d in range(1, self.depth)]
+
     def gather_all(self, unit, step):
-        y, c, x, every = self.y, self.c, self.x, slice(None)
+        y, c, z, x, every = self.y, self.c, self.z, self.x, slice(None)
         part = (
+            self.at(unit, y, c, z, x),
+            self.at(unit, y, c, z, every),
+            self.at(unit, every, c, slice(0, self.depth - 1), every),
+            self.at(unit, every, c, every, every),
+        )[step - 1] if turned(unit) else (
             self.at(unit, y, c, slice(0, self.depth - 1), x),
             self.at(unit, y, c, every, x),
             self.at(unit, y, c, every, every),
@@ -490,6 +524,16 @@
         self.gather_all(unit, step).wait_recv()
 
     def gather_sent(self, unit):
+        if not isinstance(unit, int):
+            normal = unit >= 0
+            for other in TURNED:
+                normal = normal & (unit != other)
+                pl.when(unit == other)(functools.partial(self.all_sent, other))
+            pl.when(normal)(functools.partial(self.all_sent, unit))
+        else:
+            self.all_sent(unit)
+
+    def all_sent(self, unit):
         for step in range(1, 5):
             self.gather_all(unit, step).wait_send()
 
@@ -576,7 +620,7 @@
         return [self.remote(src, dst, self.sum_sems, 4 * unit + step - 1, to) for src, dst, to in moves]
 
     def sum_all(self, unit, slot, step):
-        y, c, x, every = self.y, self.c, self.x, slice(None)
+        y, c, z, x, every = self.y, self.c, self.z, self.x, slice(None)
         src, dst = (
             (self.at(slot, every, c, every, every), self.from_core.at[unit]),
             (self.at(slot, y, c, every, every), self.from_two.at[unit]),
@@ -613,6 +657,83 @@
         for copy in self.sum_copies(unit, slot, step):
             copy.start()
 
+    def half_copies(self, half, slot, step):
+        y, c, z, x, every = self.y, self.c, self.z, self.x, slice(None)
+        to_x, to_y, to_c = self.device(x=1 - x), self.device(y=1 - y), self.device(c=1 - c)
+        lanes = pl.ds(pl.multiple_of(HALF * half, 128), HALF) if not isinstance(half, int) else pl.ds(HALF * half, HALF)
+        middle = self.depth // 2
+        near, far = slice(0, middle), slice(middle, self.depth)
+        own = pl.ds(middle * half, middle)
+        two, three, four = [a.at[LAST] for a in (self.from_two, self.from_three, self.from_four)]
+        if step == 1:
+            core = self.from_core.at[LAST, :, :, :, :, lanes]
+            moves = [(self.at(slot, every, 1 - c, every, every, lanes), core, to_c)]
+        elif step == 2:
+            moves = [
+                (self.at(slot, 1 - y, c, near, every, lanes), two.at[0, own], to_y),
+                (self.at(slot, every, c, far, 1 - x, lanes), two.at[1, own], to_x),
+            ]
+        elif step == 3:
+            moves = [
+                (self.at(slot, y, c, near, 1 - x, lanes), three.at[0, own], to_x),
+                (self.at(slot, 1 - y, c, far, x, lanes), three.at[1, own], to_y),
+            ]
+        else:
+            moves = []
+            for d in range(1, self.depth):
+                zz = self.far(d)
+                moves.append((self.at(slot, y, c, zz, x, lanes), four.at[d - 1, :, lanes], self.device(z=zz)))
+        index = 4 * (LAST + (LAST_HALF - LAST) * half) + step - 1
+        copies = [self.remote(src, dst, self.sum_sems, index, to) for src, dst, to in moves]
+        src, dst = (
+            (self.at(slot, every, c, every, every, lanes), self.from_core.at[LAST, :, :, :, :, lanes]),
+            (self.at(slot, y, c, every, every, lanes), two.at[:, own]),
+            (self.at(slot, y, c, every, x, lanes), three.at[:, own]),
+            (self.at(slot, y, c, slice(0, self.depth - 1), x, lanes), four.at[:, :, lanes]),
+        )[step - 1]
+        return copies, self.remote(src, dst, self.sum_sems, index, to_c)
+
+    def half_sent(self, half, slot):
+        for step in range(1, 5):
+            self.half_copies(half, slot, step)[1].wait_send()
+
+    def half_step(self, half, slot, step):
+        y, c, x = self.y, self.c, self.x
+        middle = self.depth // 2
+        if step > 1:
+            self.half_copies(half, slot, step - 1)[1].wait_recv()
+            lanes = slice(HALF * half, HALF * half + HALF)
+        if step == 2:
+
+            def add_one(k, carry):
+                for j in range(2):
+                    for i in range(2):
+                        self.add(self.at(slot, j, c, k, i, lanes), self.from_core.at[LAST, j, k, i, :, lanes])
+                return carry
+
+            lax.fori_loop(0, self.depth, add_one, 0)
+        elif step == 3:
+            for k in range(middle):
+                for j in range(2):
+                    low, high = self.at(slot, y, c, k, j, lanes), self.at(slot, j, c, middle + k, x, lanes)
+                    self.add(low, self.from_two.at[LAST, 0, middle * half + k, j])
+                    self.add(high, self.from_two.at[LAST, 1, middle * half + j, k])
+        elif step == 4:
+            for k in range(middle):
+                low, high = self.at(slot, y, c, k, x, lanes), self.at(slot, y, c, middle + k, x, lanes)
+                self.add(low, self.from_three.at[LAST, 0, middle * half + k])
+                self.add(high, self.from_three.at[LAST, 1, middle * half + k])
+        for copy in self.half_copies(half, slot, step)[0]:
+            copy.start()
+
+    def half_summed(self, half, slot):
+        self.half_copies(half, slot, 4)[1].wait_recv()
+        lanes = slice(HALF * half, HALF * half + HALF)
+        total = self.at(slot, self.y, self.c, self.z, self.x, lanes)[...].astype(F32)
+        for d in range(self.depth - 1):
+            total += self.from_four[LAST, d, :, lanes].astype(F32)
+        return total
+
     def summed(self, unit, slot):
         self.sum_all(unit, slot, 4).wait_recv()
         total = self.at(slot, self.y, self.c, self.z, self.x)[...].astype(F32)
@@ -629,7 +750,7 @@
         shards, vec_shard = take(2)
     else:
         weights_in, vectors_in = take(2)
-    result, input_grad = take(2)
+    result, input_grad, hidden_kept, down_kept = take(4)
     if exchanged:
         qkv_sum, out_sum, up_sum, down_sum, vec_sum = take(5)
     else:
@@ -661,14 +782,15 @@
             return weights[unit, half].reshape(HALF, WIDTH)
         return weights[unit, pl.ds(pl.multiple_of(HALF * half, HALF), HALF)]
 
-    def gradient(unit, left, right):
+    def gradient(unit, left, right, lanes=pl.ds(0, WIDTH)):
         def step(half, carry):
-            lanes = pl.ds(pl.multiple_of(HALF * half, 128), HALF)
-            values = dg(left[:, lanes], right(), 0, 0).astype(BF)
+            rows = pl.ds(pl.multiple_of(HALF * half, 128), HALF)
+            values = dg(left[:, rows], right(), 0, 0).astype(BF)
             if exchanged:
-                weights[unit, half] = values.reshape(weights.shape[2:])
+                shape = (*weights.shape[2:6], lanes.size)
+                weights[unit, half, :, :, :, :, lanes] = values.reshape(shape)
             else:
-                weights[unit, lanes] = values
+                weights[unit, rows, lanes] = values
             return carry
 
         lax.fori_loop(0, 2, step, 0)
@@ -687,8 +809,22 @@
         return jnp.sum(values.astype(F32), axis=0, keepdims=True)
 
     def copy(slot):
-        src, dst = ((tokens, x_in), (cotangent, cot), (acc_one, result), (acc_two, input_grad))[slot]
+        src, dst = ((tokens, x_in), (cotangent, cot), (low_one, result), (normed_one, input_grad))[slot]
         return pltpu.make_async_copy(src, dst, io_sems.at[slot])
+
+    hidden_homes = (normed_two, cot, low_one, mixed)
+
+    def keep_hidden(chunk):
+        return pltpu.make_async_copy(low_one, hidden_kept.at[chunk], io_sems.at[5])
+
+    def keep_down(chunk):
+        return pltpu.make_async_copy(weights.at[down(chunk)], down_kept.at[chunk], io_sems.at[6])
+
+    def fetch_hidden(chunk):
+        return pltpu.make_async_copy(hidden_kept.at[chunk], hidden_homes[chunk], io_sems.at[8 + chunk])
+
+    def fetch_down(chunk):
+        return pltpu.make_async_copy(down_kept.at[chunk], weights.at[down(chunk)], io_sems.at[12 + chunk])
 
     def place(name, turn=0):
         for index, steps in SCHEDULE.get(name, {}).items() if exchanged else ():
@@ -715,6 +851,16 @@
             ex.gather_received(unit, 4)
 
     def add_up(unit, step):
+        if unit in (LAST, LAST_HALF):
+            half = int(unit == LAST_HALF)
+            if step < 5:
+                ex.half_step(half, up(LAST), step)
+                return
+            total = ex.half_summed(half, up(LAST))
+            for part in range(3):
+                start = WIDTH * part + 256 * LAST + 128 * half
+                qkv_sum[:, start : start + 128] = total[:, 128 * part : 128 * part + 128]
+            return
         slot = up(unit) if unit < OUT else unit
         if step < 5:
             ex.sum_step(unit, slot, step)
@@ -724,8 +870,9 @@
         chunk, kind = (unit - up(0)) // 2, (unit - up(0)) % 2
         if unit < OUT:
             for part in range(3):
-                start = WIDTH * part + 256 * unit
-                qkv_sum[:, start : start + 256] = total[:, 256 * part : 256 * part + 256]
+                for half in range(2):
+                    start, own = WIDTH * part + 256 * unit + 128 * half, HALF * half + 128 * part
+                    qkv_sum[:, start : start + 128] = total[:, own : own + 128]
         elif unit == OUT:
             out_sum[...] = total
         elif kind == 0:
@@ -768,15 +915,17 @@
     def attention(unit, carry):
         place("att0", unit)
         arrived(unit)
-        bias_lanes = [pl.ds(pl.multiple_of(WIDTH * k + 256 * unit, 256), 256) for k in range(2)]
-        lanes = [pl.ds(pl.multiple_of(WIDTH * unit + 256 * k, 256), 256) for k in range(3)]
 
         def project(rows):
             full = mm(normed_one[rows], matrix(unit))
-            query = (full[:, 0:256] + fvec[2:3, bias_lanes[0]]).astype(BF).astype(F32)
-            qkv[rows, lanes[0]] = (query * HEAD**-0.5).astype(BF)
-            qkv[rows, lanes[1]] = full[:, 256:512].astype(BF)
-            qkv[rows, lanes[2]] = (full[:, 512:] + fvec[2:3, bias_lanes[1]]).astype(BF)
+            for half in range(2):
+                lanes_q, lanes_k, lanes_v = pair_lanes(unit, half)
+                start, first = HALF * half, 256 * unit + 128 * half
+                bias = [fvec[2:3, pl.ds(pl.multiple_of(b + first, 128), 128)] for b in (0, WIDTH)]
+                query = (full[:, start : start + 128] + bias[0]).astype(BF).astype(F32)
+                qkv[rows, lanes_q] = (query * HEAD**-0.5).astype(BF)
+                qkv[rows, lanes_k] = full[:, start + 128 : start + 256].astype(BF)
+                qkv[rows, lanes_v] = (full[:, start + 256 : start + HALF] + bias[1]).astype(BF)
 
         tile_loop(project, 2 * QB)
         place("att1", unit)
@@ -812,6 +961,7 @@
         place("ff0", chunk)
         arrived(up_unit)
         arrived(down_unit)
+        keep_down(chunk).start()
 
         def half_hidden(half, carry):
             lanes = pl.ds(pl.multiple_of(HALF * half, 128), HALF)
@@ -845,15 +995,16 @@
             return carry
 
         lax.fori_loop(0, 2, half_hidden, 0)
+        keep_hidden(chunk).start()
 
         def outward(rows):
-            acc_one[rows] += mm(low_one[rows], matrix(down_unit))
             acc_two[rows] += dg(low_two[rows], matrix(up_unit), 1, 1)
 
         tile_loop(outward, 2 * QB)
         place("ff3", chunk)
         if exchanged:
             ex.gather_sent(down_unit)
+        keep_down(chunk).wait()
         gradient(down_unit, low_one, lambda: cot[...])
         begin(down_unit)
         place("ff4", chunk)
@@ -862,10 +1013,11 @@
         gradient(up_unit, normed_two, lambda: low_two[...])
         begin(up_unit)
         place("ff5", chunk)
+        keep_hidden(chunk).wait()
         return carry
 
     lax.fori_loop(0, 4, feed_forward, 0)
-    copy(2).start()
+    fetch_hidden(0).start()
 
     def back_two(rows):
         normed, scale = norm_stats(residual[rows])
@@ -890,33 +1042,48 @@
     gradient(OUT, mixed, lambda: low_two[...])
     begin(OUT)
     place("dWo")
-    copy(2).wait()
     copy(0).start()
+    fetch_hidden(1).start()
 
     def attention_back(unit, carry):
-        slot = up(unit)
+        def free(slot):
+            if exchanged:
+                ex.sum_sent(slot, slot)
+            else:
+                done = pltpu.make_async_copy(weights.at[slot], weights_out.at[slot], io_sems.at[4])
+                done.start()
+                done.wait()
 
         def pair(half, carry):
             backward_pair(unit, half, qkv, mixed, low_one, lse, masks, key_acc, value_acc)
-
             place("ab0", 2 * unit + half)
+
+            @pl.when(unit == LAST)
+            def _():
+                pl.when(half == 0)(lambda: free(up(LAST)))
+                own = pl.ds(pl.multiple_of(WIDTH * LAST + HALF * half, 128), HALF)
+                lanes = pl.ds(pl.multiple_of(HALF * half, 128), HALF)
+                gradient(up(LAST), normed_one, lambda: qkv[:, own], lanes)
+                if exchanged:
+                    ex.half_step(half, up(LAST), 1)
+
             return carry
 
         lax.fori_loop(0, 2, pair, 0)
-        all_three = pl.ds(pl.multiple_of(WIDTH * unit, WIDTH), WIDTH)
-        if exchanged:
-            ex.sum_sent(slot, slot)
-        else:
-            done = pltpu.make_async_copy(weights.at[slot], weights_out.at[slot], io_sems.at[4])
-            done.start()
-            done.wait()
-        gradient(slot, normed_one, lambda: qkv[:, all_three])
-        begin(unit, slot)
+
+        @pl.when(unit != LAST)
+        def _():
+            free(up(unit))
+            all_three = pl.ds(pl.multiple_of(WIDTH * unit, WIDTH), WIDTH)
+            gradient(up(unit), normed_one, lambda: qkv[:, all_three])
+            begin(unit, up(unit))
+
         place("ab2", unit)
-        for part, row in ((0, 0), (2, WIDTH)):
-            lanes = pl.ds(pl.multiple_of(WIDTH * unit + 256 * part, 256), 256)
-            bias = pl.ds(pl.multiple_of(row + 256 * unit, 256), 256)
-            svec[2:3, bias] = tokens_sum(qkv[:, lanes])
+        for half in range(2):
+            lanes_q, _, lanes_v = pair_lanes(unit, half)
+            for row, lanes in ((0, lanes_q), (WIDTH, lanes_v)):
+                bias = pl.ds(pl.multiple_of(row + 256 * unit + 128 * half, 128), 128)
+                svec[2:3, bias] = tokens_sum(qkv[:, lanes])
 
         return carry
 
@@ -924,17 +1091,27 @@
         total = dg(qkv[rows, 0:WIDTH], matrix(0), 1, 1)
         for unit in (1, 2):
             total += dg(qkv[rows, WIDTH * unit : WIDTH * unit + WIDTH], matrix(unit), 1, 1)
-        acc_one[rows] = total
+        residual[rows] = total
         place("da1", rows.start // (2 * QB))
 
     lax.fori_loop(0, 3, attention_back, 0)
+    fetch_hidden(2).start()
+    fetch_hidden(3).start()
+    for chunk in range(4):
+        if exchanged:
+            ex.sum_sent(down(chunk), down(chunk))
+        else:
+            done = pltpu.make_async_copy(weights.at[down(chunk)], weights_out.at[down(chunk)], io_sems.at[4])
+            done.start()
+            done.wait()
+        fetch_down(chunk).start()
     tile_loop(back_qkv, 2 * QB)
     copy(0).wait()
 
     def back_one(rows):
         normed, scale = norm_stats(x_in[rows].astype(F32))
-        grad = acc_one[rows]
-        acc_two[rows] += norm_back(grad, fv(0), normed, scale)
+        grad = residual[rows]
+        normed_one[rows] = (acc_two[rows] + norm_back(grad, fv(0), normed, scale)).astype(BF)
         for row, part in ((0, grad * normed), (1, grad)):
             svec[row : row + 1, 0:WIDTH] += tokens_sum(part)
 
@@ -945,29 +1122,47 @@
         rows_to_pages(svec, ex.vec_pages.reshape(32, VEC_ROWS, 128), 32)
         ex.vector_step(3)
         place("r2p")
-        ex.vector_step(4)
+    for chunk in range(4):
+        fetch_hidden(chunk).wait()
+        fetch_down(chunk).wait()
+
+    def output(rows):
+        total = acc_one[rows]
+        for chunk, home in enumerate(hidden_homes):
+            total += mm(home[rows], matrix(down(chunk)))
+        low_one[rows] = total.astype(BF)
+        place("y", rows.start // (2 * QB))
+        if exchanged:
+            pl.when(rows.start == 0)(lambda: ex.vector_step(4))
+
+    tile_loop(output, 2 * QB)
+    copy(2).start()
+    if exchanged:
         place("drain")
         ex.vector_step(5)
         ex.vectors_sent(3, 4)
         for unit in range(3):
             ex.gather_sent(unit)
-            ex.sum_sent(unit, up(unit))
-        for unit in (OUT, up(3), *map(down, range(4))):
+            if unit != LAST:
+                ex.sum_sent(unit, up(unit))
+        for half in range(2):
+            ex.half_sent(half, up(LAST))
+        for unit in (OUT, up(3)):
             ex.sum_sent(unit, unit)
     else:
         vectors_out[...] = svec[...]
-        own = [(k, k) for k in (OUT, up(3), *map(down, range(4)))]
-        for src, dst in [(up(k), k) for k in range(3)] + own:
+        for src, dst in [(up(k), k) for k in range(3)] + [(OUT, OUT), (up(3), up(3))]:
             done = pltpu.make_async_copy(weights.at[src], weights_out.at[dst], io_sems.at[4])
             done.start()
             done.wait()
+    copy(2).wait()
     copy(3).wait()
 
 
 def finish_kernel(*refs):
     page, outs = refs[6], refs[7:]
-    outs[0][...] = refs[0][...]
-    outs[1][...] = refs[1][...]
+    outs[0][...] = refs[0][...].astype(F32)
+    outs[1][...] = refs[1][...].astype(F32)
 
     @pl.when(pl.program_id(0) == 0)
     def _():
@@ -979,13 +1174,9 @@
             jnp.concatenate([up[j, :, 4 * rows * g : 4 * rows * g + 4 * rows] for j in range(4)], 1)
             for g in range(shards // 4)
         ]
-        moved = lax.dot_general(
-            jnp.concatenate(groups, 0),
-            regroup(rows, True).astype(F32),
-            (((1,), (0,)), ((), ())),
-            preferred_element_type=F32,
-            precision=lax.Precision.HIGHEST,
-        )
+        stacked, one_hot = jnp.concatenate(groups, 0), regroup(rows, True).astype(BF)
+        high = stacked.astype(BF)
+        moved = mm(high, one_hot) + mm((stacked - high.astype(F32)).astype(BF), one_hot)
         for g in range(shards // 4):
             outs[4][:, HALF * g : HALF * g + HALF] = moved[rows * g : rows * g + rows]
         for r, dst in enumerate(outs[6:]):
@@ -1017,7 +1208,9 @@
     whole = pl.BlockSpec(memory_space=pltpu.VMEM)
     far = pl.BlockSpec(memory_space=pl.ANY)
     blocks = len(mask_blocks(length))
-    rows = [jax.ShapeDtypeStruct((length, WIDTH), F32)] * 2
+    page = (2, 2, depth, 2, weights[0].shape[1], WIDTH) if exchanged else (WIDTH, WIDTH)
+    rows = [jax.ShapeDtypeStruct((length, WIDTH), BF)] * 2
+    rows += [jax.ShapeDtypeStruct((4, length, WIDTH), BF), jax.ShapeDtypeStruct((4, *page), BF)]
     if exchanged:
         shard = weights[0].shape[1]
         in_specs = [far, far, whole, far, far]
@@ -1028,7 +1221,7 @@
             jax.ShapeDtypeStruct((4 * shard, WIDTH), F32),
             jax.ShapeDtypeStruct((VEC_ROWS, 128), F32),
         ]
-        out_specs = [far, far] + [whole] * 5
+        out_specs = [far] * 4 + [whole] * 5
         places = (2, 2, depth, 2)
         held = [vmem((UNITS, *places, shard, WIDTH), BF)]
     else:
@@ -1037,7 +1230,7 @@
             jax.ShapeDtypeStruct((UNITS, WIDTH, WIDTH), BF),
             jax.ShapeDtypeStruct((VEC_ROWS, 4 * WIDTH), F32),
         ]
-        out_specs = [far, far, far, whole]
+        out_specs = [far] * 5 + [whole]
         held = [vmem((UNITS, WIDTH, WIDTH), BF)]
     low, full = vmem((length, WIDTH), BF), vmem((length, WIDTH), F32)
     scratch = held + [
@@ -1055,7 +1248,7 @@
         low,
         vmem((VEC_ROWS, 4 * WIDTH), F32),
         vmem((VEC_ROWS, 4 * WIDTH), F32),
-        pltpu.SemaphoreType.DMA((8,)),
+        pltpu.SemaphoreType.DMA((16,)),
     ]
     if exchanged:
         dma = pltpu.SemaphoreType.DMA
@@ -1068,8 +1261,8 @@
             vmem((UNITS, depth - 1, shard, WIDTH), BF),
             dma((4 * UNITS,)),
             dma((4 * UNITS,)),
-            dma((4 * UNITS,)),
-            dma((4 * UNITS,)),
+            dma((4 * UNITS + 4,)),
+            dma((4 * UNITS + 4,)),
             dma((5,)),
             dma((5,)),
             dma((UNITS + 1,)),
@@ -1101,7 +1294,7 @@
     exchanged = mesh_shape["dp"] == 4 and mesh_shape["fsdp"] == 8 and shard % 8 == 0
     if exchanged:
         units, page = pack_layer(source_layer, vectors, matrices)
-        result, input_grad, qkv, out, wide, tall, page = run_block(
+        result, input_grad, _, _, qkv, out, wide, tall, page = run_block(
             mesh_shape, True, x_rows, c_rows, document_ids, units, page
         )
         result, input_grad, qkv, out, wide, tall, *pieces = finish(
@@ -1112,23 +1305,24 @@
         gather = lambda part: lax.all_gather(part, axes, axis=0, tiled=True)
         scatter = lambda part: lax.psum_scatter(part, axes, scatter_dimension=0, tiled=True)
         qkv, out, wide, tall = [gather(pick(m)) for m in matrices]
-        thirds = qkv.reshape(WIDTH, 3, 3, 256).transpose(2, 0, 1, 3).reshape(3, WIDTH, WIDTH)
+        thirds = qkv.reshape(WIDTH, 3, 3, 2, 128).transpose(2, 0, 3, 1, 4).reshape(3, WIDTH, WIDTH)
         ups, downs = wide.reshape(WIDTH, 4, WIDTH).transpose(1, 0, 2), tall.reshape(4, WIDTH, WIDTH)
         quarters = jnp.stack([ups, downs], 1).reshape(8, WIDTH, WIDTH)
         weights = jnp.concatenate([thirds, out[None], quarters], 0)
         rows = [gather(pick(v)).astype(F32) for v in vectors]
         table = jnp.stack([jnp.pad(r, (0, 4 * WIDTH - r.shape[0])) for r in rows])
-        result, input_grad, weights, table = run_block(
+        result, input_grad, _, _, weights, table = run_block(
             mesh_shape, False, x_rows, c_rows, document_ids, weights, table
         )
         weights = weights.astype(F32)
-        qkv = weights[0:3].reshape(3, WIDTH, 3, 256).transpose(1, 2, 0, 3).reshape(WIDTH, -1)
+        qkv = weights[0:3].reshape(3, WIDTH, 2, 3, 128).transpose(1, 3, 0, 2, 4).reshape(WIDTH, -1)
         wide = weights[up(0) :: 2].transpose(1, 0, 2).reshape(WIDTH, -1)
         tall = weights[down(0) :: 2].reshape(4 * WIDTH, WIDTH)
         qkv, out, wide, tall = [scatter(m) for m in (qkv, weights[OUT], wide, tall)]
         pieces = [scatter(table[r, 0 : WIDTH * s]) for r, s in enumerate(VEC_SIZES)]
     gain, shift, qv, outb, mid_gain, mid_shift, upb, downb = pieces
     shape = tokens.shape
+    result, input_grad = result.astype(F32), input_grad.astype(F32)
     return (
         result.reshape(shape),
         input_grad.reshape(shape),

time: 170 us -> 162 us (0.953)
  Pallas kernels: 168 us -> 160 us
    pallas_call x1, Pallas kernels: 159 us -> 153 us  [run_block(): pl.pallas_call(functools.partial(block_kernel, mesh_shape, exchanged), ou...]
where the time goes in v1:
time: 162 us
  Pallas kernels  160 us (99%)
    pallas_call x1, Pallas kernels, run_block(): pl.pallas_call(functools.partial(block_kernel, mesh_shape, exchanged), ou...  153 us
    pallas_call x1, Pallas kernels, finish(): pl.pallas_call(finish_kernel, grid=(2,), in_specs=ins, out_specs=outs, ou...  5.34 us

profile of v1, /device:TPU:0, one launch (start us, length us, event | category | flops | bytes accessed | tf_op | source)
XLA Modules:
  0.0 161.7 jit_solution(2065174950493840666)
XLA Ops:
  1.3 2.3 %pick_layer.1 = (bf16[12,24,768]{2,1,0:T(8,128)(2,1)}, f32[8,128]{1,0:T(8,128)}) custom-call(s32[1]{0:T(128)} %bitcast.5.layer_ref, bf16[12,24]{1,0:T(8,128)(2,1)} %refs_0_.1, bf16[12,24]{1,0:T(8,128)(2,1)} %refs_1_.1, bf16[12,48]{1,0:T(8,128)(2,1)} %refs_2_.2, bf16[12,24]{1,0:T(8,128)(2,1)} %refs_3_.1, bf16[12,24]{1,0:T(8,128)(2,1)} %refs_4_.1, ...), custom_call_target="tpu_custom_call" | custom-call | tf_op jit(solution)/shard_map/pick_layer/pallas_call | solution.py:186
  3.6 152.6 %block.1 = (bf16[1024,768]{1,0:T(8,128)(2,1)}, bf16[1024,768]{1,0:T(8,128)(2,1)}, bf16[4,1024,768]{2,1,0:T(8,128)(2,1)}, bf16[4,2,2,4,2,24,768]{6,5,4,3,2,1,0:T(...) custom-call(bf16[1024,768]{1,0:T(8,128)(2,1)} %bitcast.6, ...), custom_call_target="tpu_custom_call" | custom-call | tf_op jit(solution)/shard_map/block/pallas_call | solution.py:1273
  156.2 5.3 %finish.1 = (f32[1024,768]{1,0:T(8,128)}, f32[1024,768]{1,0:T(8,128)}, f32[24,2304]{1,0:T(8,128)}, f32[24,768]{1,0:T(8,128)}, f32[24,3072]{1,0:T(8,128)}, /*inde...) custom-call(bf16[1024,768]{1,0:T(8,128)(2,1)} %get-tuple-element.39., ...), custom_call_target="tpu_custom_call" | custom-call | tf_op jit(solution)/shard_map/finish/pallas_call | solution.py:1194

commit v2 on v1

--- a/solution.py
+++ b/solution.py
@@ -18,6 +18,7 @@
 HALF = 384
 HEAD = 64
 QB = 256
+DOCS = 4
 VEC_ROWS = 8
 VMEM_BYTES = 63 * 2**20
 VEC_SIZES = (1, 1, 2, 1, 1, 1, 4, 1)
@@ -35,86 +36,80 @@
 
 
 SCHEDULE = {
-    "rows": {
+    "vec": {
         0: ((0, 0, 2),),
     },
     "att0": {
-        0: ((0, 1, 2), (0, 0, 3), (0, 2, 2), (0, 1, 3), (0, 3, 2), (0, 0, 4), (0, 2, 3), (0, 6, 2),),
+        0: ((0, 1, 2), (0, 0, 3), (0, 2, 2), (0, 1, 3), (0, 3, 2), (0, 0, 4), (0, 2, 3),),
     },
     "att1": {
         0: ((0, 4, 2),),
+        2: ((0, 3, 4),),
     },
     "att2": {
         0: ((0, 1, 4),),
-        1: ((0, 3, 3), (0, 5, 2),),
-        2: ((0, 2, 4), (0, 6, 3), (0, 7, 2),),
-        3: ((0, 4, 3), (0, 8, 2),),
-        4: ((0, 3, 4),),
-        5: ((0, 5, 3), (0, 7, 3), (0, 9, 2), (0, 10, 2),),
+        1: ((0, 3, 3), (0, 5, 2), (0, 6, 2),),
+        2: ((0, 2, 4), (0, 4, 3), (0, 7, 2),),
+        4: ((0, 5, 3), (0, 6, 3), (0, 8, 2), (0, 9, 2),),
     },
     "attended": {
-        0: ((0, 11, 2),),
-    },
-    "masksT": {
         0: ((0, 4, 4),),
     },
     "ff0": {
-        0: ((0, 8, 3), (0, 5, 4),),
+        0: ((0, 7, 3), (0, 10, 2), (0, 5, 4), (0, 8, 3), (0, 11, 2),),
     },
     "ff1": {
-        0: ((0, 7, 4),),
-        1: ((0, 9, 3),),
-        2: ((0, 8, 4), (1, 5, 2), (1, 4, 2),),
-        3: ((0, 9, 4),),
-        4: ((1, 5, 3), (1, 7, 2),),
-        5: ((0, 10, 4), (1, 4, 3), (1, 6, 2),),
-        6: ((1, 4, 4), (1, 9, 2), (1, 8, 2), (1, 5, 5),),
+        0: ((0, 9, 3),),
+        2: ((0, 8, 4), (0, 11, 3), (1, 5, 2), (1, 4, 2),),
+        4: ((1, 7, 2), (1, 5, 3), (1, 6, 2),),
+        5: ((0, 10, 4),),
+        6: ((1, 8, 2),),
         7: ((1, 6, 3),),
     },
     "ff3": {
-        0: ((0, 6, 4), (0, 10, 3),),
-        2: ((1, 5, 4),),
+        0: ((0, 7, 4), (0, 6, 4),),
+        1: ((0, 9, 4),),
+        2: ((1, 4, 3),),
+        3: ((1, 4, 4), (1, 5, 5),),
+    },
+    "ff4": {
+        0: ((0, 10, 3),),
         3: ((1, 7, 4),),
     },
-    "ff4": {
-        0: ((0, 11, 3),),
+    "ff5": {
         1: ((0, 11, 4),),
-        3: ((1, 4, 5),),
-    },
-    "ff5": {
-        2: ((1, 7, 3),),
-        3: ((1, 9, 3),),
+        2: ((1, 7, 3), (1, 9, 2), (1, 5, 4),),
+        3: ((1, 9, 3), (1, 11, 2),),
     },
     "back_two": {
-        0: ((1, 8, 3), (1, 11, 2), (1, 6, 4), (1, 10, 2), (1, 7, 5),),
+        0: ((1, 8, 3), (1, 10, 2), (1, 4, 5),),
     },
     "back_out": {
+        0: ((1, 6, 4), (1, 7, 5),),
+    },
+    "dWo": {
         0: ((1, 9, 4),),
     },
-    "dWo": {
-        0: ((1, 8, 4),),
-    },
     "ab0": {
-        0: ((1, 11, 3), (1, 3, 2), (1, 6, 5),),
+        0: ((1, 11, 3), (1, 3, 2), (1, 8, 4), (1, 6, 5),),
         1: ((1, 10, 3), (1, 9, 5),),
-        2: ((1, 10, 4), (1, 3, 3), (1, 0, 2),),
-        3: ((1, 11, 5),),
-        4: ((1, 0, 3), (1, 1, 2),),
+        2: ((1, 3, 3), (1, 0, 2), (1, 8, 5),),
+        3: ((1, 10, 4), (1, 3, 4), (1, 11, 5),),
+        4: ((1, 0, 3), (1, 1, 2), (1, 10, 5),),
         5: ((1, 0, 4), (1, 2, 2), (1, 3, 5),),
     },
     "ab2": {
-        0: ((1, 11, 4), (1, 8, 5),),
-        1: ((1, 3, 4), (1, 10, 5),),
+        0: ((1, 11, 4),),
     },
     "da1": {
-        0: ((1, 1, 3), (1, 12, 2), (1, 2, 3),),
+        0: ((1, 1, 3), (1, 2, 3), (1, 12, 2),),
         1: ((1, 0, 5),),
     },
     "back_one": {
-        0: ((1, 1, 4),),
+        0: ((1, 1, 4), (1, 2, 4),),
     },
     "r2p": {
-        0: ((1, 12, 3), (1, 2, 4),),
+        0: ((1, 12, 3),),
     },
     "y": {
         0: ((1, 12, 4),),
@@ -271,33 +266,28 @@
     return [(max(0, i * QB - reach), (i + 1) * QB) for i in range(length // QB)]
 
 
-def mask_blocks(length):
-    blocks = {}
-    for i, (lo, hi) in enumerate(key_ranges(length)):
-        for key in range(lo, hi, QB):
-            blocks[i, key // QB] = len(blocks)
-    return blocks
-
-
-def build_masks(doc_ref, masks, transposed):
+def build_masks(doc_ref, causal, features):
+    for by_key in range(2):
+        q_pos = lax.broadcasted_iota(jnp.int32, (QB, QB), by_key)
+        k_pos = lax.broadcasted_iota(jnp.int32, (QB, QB), 1 - by_key)
+        causal[by_key] = jnp.where(k_pos <= q_pos, 0.0, NEG_LARGE)
     length = doc_ref.shape[1]
-    row = doc_ref[...].astype(F32)
-    for (i, b), at in mask_blocks(length).items():
-        queries = row[:, i * QB : (i + 1) * QB]
-        keys = row[:, b * QB : (b + 1) * QB]
-        along, down = (queries, keys) if transposed else (keys, queries)
-        down = jnp.transpose(jnp.broadcast_to(down, (128, QB)))
-        down = jnp.concatenate([down, down], 1)
-        q_dim = 1 if transposed else 0
-        q_pos = lax.broadcasted_iota(jnp.int32, (QB, QB), q_dim) + i * QB
-        k_pos = lax.broadcasted_iota(jnp.int32, (QB, QB), 1 - q_dim) + b * QB
-        masks[at] = jnp.where((k_pos <= q_pos) & (down == along), 0.0, NEG_LARGE)
-
-
-def head_lanes(values, head, other=0.0):
+    own = jnp.transpose(jnp.broadcast_to(doc_ref[...].astype(F32), (128, length)))
+    lane = lax.broadcasted_iota(jnp.int32, (length, 128), 1)
+    lane = jnp.where(lane >= HEAD, lane - HEAD, lane).astype(F32)
+    same = own == lane
+    features[0] = jnp.where(same | (lane >= DOCS), 0.0, NEG_LARGE).astype(BF)
+    features[1] = jnp.where(same, 1.0, 0.0).astype(BF)
+
+
+def head_lanes(values, head, other):
     lane = lax.broadcasted_iota(jnp.int32, values.shape, 1)
     keep = lane >= HEAD if head else lane < HEAD
-    return jnp.where(keep, values, jnp.full(values.shape, other, values.dtype))
+    return jnp.where(keep, values, other)
+
+
+def alone(values, head, fill=0.0):
+    return head_lanes(values, head, jnp.full(values.shape, fill, values.dtype))
 
 
 def pair_lanes(unit, half):
@@ -305,10 +295,11 @@
     return [pl.ds(pl.multiple_of(s, 128), 128) for s in start]
 
 
-def forward_pair(unit, half, qkv, mixed, lse, masks):
+def forward_pair(unit, half, qkv, mixed, lse, causal, features):
     length = qkv.shape[0]
     lanes_q, lanes_k, lanes_v = pair_lanes(unit, half)
-    ranges, blocks = key_ranges(length), mask_blocks(length)
+    ranges = key_ranges(length)
+    keys = [head_lanes(qkv[:, lanes_k], h, features[1]) for h in range(2)]
     pair = 2 * unit + half
     lanes_o = pl.ds(pl.multiple_of(pair * 128, 128), 128)
     steps = [(i, h) for i in range(len(ranges)) for h in range(2)]
@@ -317,16 +308,16 @@
         i, h = step
         lo, hi = ranges[i]
         rows = slice(i * QB, (i + 1) * QB)
-        raw = dg(head_lanes(qkv[rows, lanes_q], h), qkv[lo:hi, lanes_k], 1, 1)
-        mask = [masks[blocks[i, b]] for b in range(lo // QB, hi // QB)]
-        return raw + jnp.concatenate(mask, 1)
+        raw = dg(head_lanes(qkv[rows, lanes_q], h, features[0, rows]), keys[h][lo:hi], 1, 1)
+        last = raw[:, hi - lo - QB :] + causal[0]
+        return jnp.concatenate([raw[:, : hi - lo - QB], last], 1) if hi - lo > QB else last
 
     def finish(step, score):
         i, h = step
         lo, hi = ranges[i]
         top = jnp.max(score, axis=1, keepdims=True)
         soft = jnp.exp(score - top).astype(BF)
-        return mm(soft, head_lanes(qkv[lo:hi, lanes_v], h, 1.0)), top
+        return mm(soft, alone(qkv[lo:hi, lanes_v], h, 1.0)), top
 
     current, done = scores(steps[0]), {}
     for n, step in enumerate(steps):
@@ -345,10 +336,11 @@
             lse[pair, 1:2, rows] = logs[HEAD : HEAD + 1]
 
 
-def backward_pair(unit, half, qkv, mixed, mixed_grad, lse, masks, key_acc, value_acc):
+def backward_pair(unit, half, qkv, mixed, mixed_grad, lse, causal, features, key_acc, value_acc):
     length = qkv.shape[0]
     lanes_q, lanes_k, lanes_v = pair_lanes(unit, half)
-    ranges, blocks = key_ranges(length), mask_blocks(length)
+    ranges = key_ranges(length)
+    keys = [head_lanes(qkv[:, lanes_k], h, features[1]) for h in range(2)]
     pair = 2 * unit + half
     lanes_o = pl.ds(pl.multiple_of(pair * 128, 128), 128)
     keys_t = jnp.transpose(qkv[:, lanes_k])
@@ -359,10 +351,11 @@
         i, h = step
         lo, hi = ranges[i]
         rows = slice(i * QB, (i + 1) * QB)
-        query = head_lanes(qkv[rows, lanes_q], h)
-        grad = head_lanes(mixed_grad[rows, lanes_o], h)
-        mask = [masks[blocks[i, b]] for b in range(lo // QB, hi // QB)]
-        score = dg(qkv[lo:hi, lanes_k], query, 1, 1) + jnp.concatenate(mask, 0)
+        query = alone(qkv[rows, lanes_q], h)
+        grad = alone(mixed_grad[rows, lanes_o], h)
+        raw = dg(keys[h][lo:hi], head_lanes(qkv[rows, lanes_q], h, features[0, rows]), 1, 1)
+        last = raw[hi - lo - QB :] + causal[1]
+        score = jnp.concatenate([raw[: hi - lo - QB], last], 0) if hi - lo > QB else last
         return score, dg(qkv[lo:hi, lanes_v], grad, 1, 1), query, grad
 
     def finish(step, started):
@@ -396,12 +389,12 @@
             lo, hi = ranges[i]
             query_grad = jnp.transpose(jnp.concatenate([q0, q1], 0))
             qkv[rows, lanes_q] = (query_grad * HEAD**-0.5).astype(BF)
-            keys, values, old = k0 + k1, v0 + v1, hi - QB - lo
+            key_part, value_part, old = k0 + k1, v0 + v1, hi - QB - lo
             if old:
-                key_acc[lo : lo + old] += keys[:old]
-                value_acc[lo : lo + old] += values[:old]
-            key_acc[hi - QB : hi] = keys[old:]
-            value_acc[hi - QB : hi] = values[old:]
+                key_acc[lo : lo + old] += key_part[:old]
+                value_acc[lo : lo + old] += value_part[:old]
+            key_acc[hi - QB : hi] = key_part[old:]
+            value_acc[hi - QB : hi] = value_part[old:]
     qkv[:, lanes_k] = key_acc[...].astype(BF)
     qkv[:, lanes_v] = value_acc[...].astype(BF)
 
@@ -593,7 +586,7 @@
             self.vector_all(step).wait_send()
 
     def add(self, place, other):
-        place[...] = (place[...].astype(F32) + other[...].astype(F32)).astype(BF)
+        place[...] = place[...] + other[...]
 
     def sum_copies(self, unit, slot, step):
         y, c, z, x = self.y, self.c, self.z, self.x
@@ -755,7 +748,7 @@
         qkv_sum, out_sum, up_sum, down_sum, vec_sum = take(5)
     else:
         weights_out, vectors_out = take(2)
-    (weights, cot, normed_one, qkv, mixed, lse, masks, residual, normed_two) = take(9)
+    (weights, cot, normed_one, qkv, mixed, lse, causal, features, residual, normed_two) = take(10)
     (acc_one, acc_two, low_one, low_two, fvec, svec, io_sems) = take(7)
     x_in = low_two
     key_acc, value_acc = residual.at[:, 0:128], residual.at[:, 128:256]
@@ -888,7 +881,7 @@
         ex.vector_step(1)
         for unit in range(UNITS):
             ex.gather_step(unit, 1)
-        build_masks(documents, masks, False)
+        build_masks(documents, causal, features)
         place("masks")
         ex.vector_step(2)
         place("vec")
@@ -899,7 +892,7 @@
     else:
         weights_copy = pltpu.make_async_copy(weights_in, weights, io_sems.at[4])
         weights_copy.start()
-        build_masks(documents, masks, False)
+        build_masks(documents, causal, features)
         fvec[...] = vectors_in[...]
     copy(0).wait()
 
@@ -931,7 +924,7 @@
         place("att1", unit)
 
         def pair(half, carry):
-            forward_pair(unit, half, qkv, mixed, lse, masks)
+            forward_pair(unit, half, qkv, mixed, lse, causal, features)
             place("att2", 2 * unit + half)
             return carry
 
@@ -951,10 +944,8 @@
         acc_one[rows] = total + fv(7)
         acc_two[rows] = jnp.zeros_like(total)
 
-    tile_loop(attend)
+    tile_loop(attend, 2 * QB)
     place("attended")
-    build_masks(documents, masks, True)
-    place("masksT")
 
     def feed_forward(chunk, carry):
         up_unit, down_unit = up(chunk), down(chunk)
@@ -977,11 +968,12 @@
                 square = pre * pre
                 bent = jnp.tanh(pre * (GELU_COEF + (GELU_COEF * GELU_CUBIC) * square))
                 upper = 0.5 + 0.5 * bent
-                slope = upper + (0.5 * pre) * (1.0 - bent * bent) * (
-                    GELU_COEF + (3.0 * GELU_COEF * GELU_CUBIC) * square
+                value = pre * upper
+                slope = upper + (value - value * upper) * (
+                    2.0 * GELU_COEF + (6.0 * GELU_COEF * GELU_CUBIC) * square
                 )
                 rows = slice(start, start + QB)
-                low_one[rows, lanes] = (pre * upper).astype(BF)
+                low_one[rows, lanes] = value.astype(BF)
                 back = (grad * slope).astype(BF)
                 low_two[rows, lanes] = back
                 svec[6:7, wide] += tokens_sum(back)
@@ -1055,7 +1047,7 @@
                 done.wait()
 
         def pair(half, carry):
-            backward_pair(unit, half, qkv, mixed, low_one, lse, masks, key_acc, value_acc)
+            backward_pair(unit, half, qkv, mixed, low_one, lse, causal, features, key_acc, value_acc)
             place("ab0", 2 * unit + half)
 
             @pl.when(unit == LAST)
@@ -1126,6 +1118,10 @@
         fetch_hidden(chunk).wait()
         fetch_down(chunk).wait()
 
+    def sent_rows(rows):
+        sem = io_sems.at[2 + 5 * (rows.start // (2 * QB))]
+        return pltpu.make_async_copy(low_one.at[rows], result.at[rows], sem)
+
     def output(rows):
         total = acc_one[rows]
         for chunk, home in enumerate(hidden_homes):
@@ -1134,9 +1130,9 @@
         place("y", rows.start // (2 * QB))
         if exchanged:
             pl.when(rows.start == 0)(lambda: ex.vector_step(4))
+        sent_rows(rows).start()
 
     tile_loop(output, 2 * QB)
-    copy(2).start()
     if exchanged:
         place("drain")
         ex.vector_step(5)
@@ -1155,7 +1151,8 @@
             done = pltpu.make_async_copy(weights.at[src], weights_out.at[dst], io_sems.at[4])
             done.start()
             done.wait()
-    copy(2).wait()
+    for start in range(0, length, 2 * QB):
+        sent_rows(pl.ds(start, 2 * QB)).wait()
     copy(3).wait()
 
 
@@ -1207,7 +1204,6 @@
     vmem = pltpu.VMEM
     whole = pl.BlockSpec(memory_space=pltpu.VMEM)
     far = pl.BlockSpec(memory_space=pl.ANY)
-    blocks = len(mask_blocks(length))
     page = (2, 2, depth, 2, weights[0].shape[1], WIDTH) if exchanged else (WIDTH, WIDTH)
     rows = [jax.ShapeDtypeStruct((length, WIDTH), BF)] * 2
     rows += [jax.ShapeDtypeStruct((4, length, WIDTH), BF), jax.ShapeDtypeStruct((4, *page), BF)]
@@ -1239,7 +1235,8 @@
         vmem((length, 3 * WIDTH), BF),
         low,
         vmem((6, 8, length), F32),
-        vmem((blocks, QB, QB), F32),
+        vmem((2, QB, QB), F32),
+        vmem((2, length, 128), BF),
         full,
         low,
         full,

time: 162 us -> 159 us (0.981)
  Pallas kernels: 160 us -> 157 us
    pallas_call x1, Pallas kernels: 153 us -> 150 us  [run_block(): pl.pallas_call(functools.partial(block_kernel, mesh_shape, exchanged), ou...]
where the time goes in v2:
time: 159 us
  Pallas kernels  157 us (99%)
    pallas_call x1, Pallas kernels, run_block(): pl.pallas_call(functools.partial(block_kernel, mesh_shape, exchanged), ou...  150 us
    pallas_call x1, Pallas kernels, finish(): pl.pallas_call(finish_kernel, grid=(2,), in_specs=ins, out_specs=outs, ou...  5.34 us

profile of v2, /device:TPU:0, one launch (start us, length us, event | category | flops | bytes accessed | tf_op | source)
XLA Modules:
  0.0 158.7 jit_solution(15284517258513400486)
XLA Ops:
  1.3 2.3 %pick_layer.1 = (bf16[12,24,768]{2,1,0:T(8,128)(2,1)}, f32[8,128]{1,0:T(8,128)}) custom-call(s32[1]{0:T(128)} %bitcast.5.layer_ref, bf16[12,24]{1,0:T(8,128)(2,1)} %refs_0_.1, bf16[12,24]{1,0:T(8,128)(2,1)} %refs_1_.1, bf16[12,48]{1,0:T(8,128)(2,1)} %refs_2_.2, bf16[12,24]{1,0:T(8,128)(2,1)} %refs_3_.1, bf16[12,24]{1,0:T(8,128)(2,1)} %refs_4_.1, ...), custom_call_target="tpu_custom_call" | custom-call | tf_op jit(solution)/shard_map/pick_layer/pallas_call | solution.py:181
  3.6 149.6 %block.1 = (bf16[1024,768]{1,0:T(8,128)(2,1)}, bf16[1024,768]{1,0:T(8,128)(2,1)}, bf16[4,1024,768]{2,1,0:T(8,128)(2,1)}, bf16[4,2,2,4,2,24,768]{6,5,4,3,2,1,0:T(...) custom-call(bf16[1024,768]{1,0:T(8,128)(2,1)} %bitcast.6, ...), custom_call_target="tpu_custom_call" | custom-call | tf_op jit(solution)/shard_map/block/pallas_call | solution.py:1270
  153.2 5.3 %finish.1 = (f32[1024,768]{1,0:T(8,128)}, f32[1024,768]{1,0:T(8,128)}, f32[24,2304]{1,0:T(8,128)}, f32[24,768]{1,0:T(8,128)}, f32[24,3072]{1,0:T(8,128)}, /*inde...) custom-call(bf16[1024,768]{1,0:T(8,128)(2,1)} %get-tuple-element.39., ...), custom_call_target="tpu_custom_call" | custom-call | tf_op jit(solution)/shard_map/finish/pallas_call | solution.py:1191

commit v3 on v2

--- a/solution.py
+++ b/solution.py
@@ -878,13 +878,18 @@
     svec[...] = jnp.zeros(svec.shape, F32)
     if exchanged:
         ex.barrier()
+        ex.gather_step(0, 1)
         ex.vector_step(1)
-        for unit in range(UNITS):
+        early = (1, 2, 3, *TURNED)
+        for unit in early:
             ex.gather_step(unit, 1)
         build_masks(documents, causal, features)
         place("masks")
         ex.vector_step(2)
         place("vec")
+        for unit in range(1, UNITS):
+            if unit not in early:
+                ex.gather_step(unit, 1)
         ex.vector_all(2).wait_recv()
         ex.vectors_sent(1, 2)
         pages_to_rows(ex.vec_pages.reshape(32, VEC_ROWS, 128), fvec, 32)
@@ -920,7 +925,7 @@
                 qkv[rows, lanes_k] = full[:, start + 128 : start + 256].astype(BF)
                 qkv[rows, lanes_v] = (full[:, start + 256 : start + HALF] + bias[1]).astype(BF)
 
-        tile_loop(project, 2 * QB)
+        tile_loop(project, length)
         place("att1", unit)
 
         def pair(half, carry):
@@ -992,7 +997,7 @@
         def outward(rows):
             acc_two[rows] += dg(low_two[rows], matrix(up_unit), 1, 1)
 
-        tile_loop(outward, 2 * QB)
+        tile_loop(outward, length)
         place("ff3", chunk)
         if exchanged:
             ex.gather_sent(down_unit)

time: 159 us -> 158 us (level)
  no operation moved by 1% of the time
where the time goes in v3:
time: 158 us
  Pallas kernels  156 us (99%)
    pallas_call x1, Pallas kernels, run_block(): pl.pallas_call(functools.partial(block_kernel, mesh_shape, exchanged), ou...  149 us
    pallas_call x1, Pallas kernels, finish(): pl.pallas_call(finish_kernel, grid=(2,), in_specs=ins, out_specs=outs, ou...  5.34 us

profile of v3, /device:TPU:0, one launch (start us, length us, event | category | flops | bytes accessed | tf_op | source)
XLA Modules:
  0.0 157.8 jit_solution(2408348320286743049)
XLA Ops:
  1.3 2.3 %pick_layer.1 = (bf16[12,24,768]{2,1,0:T(8,128)(2,1)}, f32[8,128]{1,0:T(8,128)}) custom-call(s32[1]{0:T(128)} %bitcast.5.layer_ref, bf16[12,24]{1,0:T(8,128)(2,1)} %refs_0_.1, bf16[12,24]{1,0:T(8,128)(2,1)} %refs_1_.1, bf16[12,48]{1,0:T(8,128)(2,1)} %refs_2_.2, bf16[12,24]{1,0:T(8,128)(2,1)} %refs_3_.1, bf16[12,24]{1,0:T(8,128)(2,1)} %refs_4_.1, ...), custom_call_target="tpu_custom_call" | custom-call | tf_op jit(solution)/shard_map/pick_layer/pallas_call | solution.py:181
  3.6 148.7 %block.1 = (bf16[1024,768]{1,0:T(8,128)(2,1)}, bf16[1024,768]{1,0:T(8,128)(2,1)}, bf16[4,1024,768]{2,1,0:T(8,128)(2,1)}, bf16[4,2,2,4,2,24,768]{6,5,4,3,2,1,0:T(...) custom-call(bf16[1024,768]{1,0:T(8,128)(2,1)} %bitcast.6, ...), custom_call_target="tpu_custom_call" | custom-call | tf_op jit(solution)/shard_map/block/pallas_call | solution.py:1275
  152.3 5.3 %finish.1 = (f32[1024,768]{1,0:T(8,128)}, f32[1024,768]{1,0:T(8,128)}, f32[24,2304]{1,0:T(8,128)}, f32[24,768]{1,0:T(8,128)}, f32[24,3072]{1,0:T(8,128)}, /*inde...) custom-call(bf16[1024,768]{1,0:T(8,128)(2,1)} %get-tuple-element.39., ...), custom_call_target="tpu_custom_call" | custom-call | tf_op jit(solution)/shard_map/finish/pallas_call | solution.py:1196
